TPU v7x, 256 devices: a whole 4x4x8 slice. The times are simulated.
256 devices in a mesh: lat: 16 (over z, y_lo), lay: 16 (over y_hi, x, core).
Axes of the slice: x: 4, y: 4 (y_hi: 2, y_lo: 2; y = y_hi * 2 + y_lo), z: 8, core: 2. Of those that a mesh axis runs over, the one named last changes fastest.
Arguments:
- wave_field: float32 [2, 128, 512, 512], P(None, 'lay', 'lat'), may hold values from -6 to 6
- contrast: float32 [128, 512, 512], P('lay', 'lat'), may hold values from 0.1 to 1.5
- layer_of_plane: int32 [128], replicated, may hold values from 0 to 7, never falling along the last dimension, each value on 1 to 32 neighbouring positions
- toeplitz_table: float32 [2, 8, 255], replicated, may hold values from -0.5 to 0.5
- hankel_table: float32 [2, 8, 255], replicated, may hold values from -0.5 to 0.5
- layer_rates: float32 [8], replicated, may hold values from 0.5 to 1.5
Outputs:
- scattered_field: float32 [2, 128, 512, 512], P(None, 'lay', 'lat')
Inputs may be any that keep to these rules, and one draw needn't show every extreme that they name: `layer_of_plane`: layer numbers never fall from one plane to the next; every layer holds 1 to 32 planes.
All inputs are finite; a program needn't handle non-finite values.
Results may differ from a plain program's by a relative error of at most 0.00007.
Values sent between devices are 32-bit elements; how exact they have to be, the bound alone decides.
No kernel may reach another device: no remote copies, remote signals or barrier semaphores. Data moves between devices by JAX's collectives and lax.ppermute only.
A program may use at most 128 MiB of HBM per device.

v0:
```python
import functools
import math

import jax
import jax.numpy as jnp
import numpy as np
import ml_dtypes
from jax import lax
from jax.experimental import pallas as pl
from jax.experimental.pallas import tpu as pltpu
from jax.sharding import PartitionSpec as P

AXES = ("lay", "lat")
F32 = jnp.float32
BF16 = jnp.bfloat16
HALF = 256
PLANES = 128
LAYERS = 8
MIB = 1 << 20


def split_np(x):
    x = x.astype(np.float32)
    hi = x.astype(ml_dtypes.bfloat16)
    lo = (x - hi.astype(np.float32)).astype(ml_dtypes.bfloat16)
    return hi, lo


def dft_tables():
    index = np.arange(HALF)
    angle = 2.0 * math.pi / HALF * ((index[:, None] * index[None, :]) % HALF)
    hi, lo = split_np(np.concatenate([np.cos(angle), np.sin(angle)], 0))
    turn = 2.0 * math.pi / (2 * HALF) * index
    return hi, lo, np.stack([np.cos(turn), np.sin(turn)]).astype(np.float32)


def split(x):
    hi = x.astype(BF16)
    return hi, (x - hi.astype(F32)).astype(BF16)


def dot_nt(a, b):
    return lax.dot_general(a, b, (((1,), (1,)), ((), ())), preferred_element_type=F32)


def dot3(a_hi, a_lo, b_hi, b_lo):
    return dot_nt(a_hi, b_hi) + dot_nt(a_hi, b_lo) + dot_nt(a_lo, b_hi)


def forward_y_kernel(w_ref, hi_ref, lo_ref, tw_ref, o_ref):
    cos, sin = tw_ref[0:1, :], tw_ref[1:2, :]
    t_hi, t_lo = hi_ref[...], lo_ref[...]
    lane = lax.broadcasted_iota(jnp.int32, (HALF, 128), 1)
    planes = w_ref.shape[1]
    for pair in range(planes // 2):
        rows = []
        for z in (2 * pair, 2 * pair + 1):
            first = [w_ref[c, z, :, :HALF] for c in (0, 1)]
            second = [w_ref[c, z, :, HALF:] for c in (0, 1)]
            even = [first[c] + second[c] for c in (0, 1)]
            odd = [first[c] - second[c] for c in (0, 1)]
            odd_re = odd[0] * cos + odd[1] * sin
            odd_im = odd[1] * cos - odd[0] * sin
            rows += [even[0], odd_re, even[1], odd_im]
        v_hi, v_lo = split(jnp.concatenate(rows, 0))
        out = dot3(t_hi, t_lo, v_hi, v_lo)
        for k in (0, 1):
            with_cos = out[:HALF, 128 * k : 128 * (k + 1)]
            with_sin = pltpu.roll(out[HALF:, 128 * k : 128 * (k + 1)], 64, 1)
            o_ref[pl.ds(2 * pair + k, HALF, stride=8), :] = with_cos + jnp.where(lane < 64, with_sin, -with_sin)


def tables_kernel(layer_ref, toe_ref, han_ref, r_ref):
    layer_rows = jnp.transpose(jnp.broadcast_to(layer_ref[...].astype(F32), (PLANES, PLANES)))
    wide = jnp.concatenate([layer_rows, layer_rows], 1)
    row = lax.broadcasted_iota(jnp.int32, (PLANES, 2 * PLANES), 0)

    def spread(ref, c, amount):
        x = jnp.zeros((PLANES, 2 * PLANES), F32)
        for l in range(LAYERS):
            x = jnp.where(wide == float(l), ref[c, l : l + 1, :], x)
        for bit in range(7):
            moved = pltpu.roll(x, 2 * PLANES - (1 << bit), 1)
            x = jnp.where(((amount >> bit) & 1) == 1, moved, x)
        return x[:, :PLANES]

    toe = [spread(toe_ref, c, PLANES - 1 - row) for c in (0, 1)]
    han = [spread(han_ref, c, row) for c in (0, 1)]
    z = lax.broadcasted_iota(jnp.int32, (PLANES, PLANES), 0)
    s = lax.broadcasted_iota(jnp.int32, (PLANES, PLANES), 1)
    low = [jnp.where(s <= z, x, 0.0) for x in toe]
    high = [jnp.where(s > z, x, 0.0) for x in toe]
    for t, (re, im) in enumerate((low, high, han)):
        for out_part, blocks in enumerate(((re, -im), (im, re))):
            for in_part, block in enumerate(blocks):
                hi = block.astype(BF16).astype(F32)
                lo = block - hi
                for l in range(LAYERS):
                    here = layer_rows == float(l)
                    rows = slice(PLANES * out_part, PLANES * (out_part + 1))
                    at = 2 * PLANES * l + PLANES * in_part
                    r_ref[2 * t, rows, at : at + PLANES] = jnp.where(here, hi, 0.0).astype(BF16)
                    r_ref[2 * t + 1, rows, at : at + PLANES] = jnp.where(here, lo, 0.0).astype(BF16)


def exchange(parts):
    piece = lax.broadcasted_iota(jnp.int32, parts[0].shape, 1) // 32
    turned = [x if i == 0 else pltpu.roll(x, 32 * i, 1) for i, x in enumerate(parts)]
    out = []
    for q in range(4):
        x = turned[(3 - q) % 4]
        for p in range(3):
            x = jnp.where(piece == p, turned[(p - q) % 4], x)
        out.append(x if q == 0 else pltpu.roll(x, 128 - 32 * q, 1))
    return out


def middle_kernel(
    rates_ref, ky_ref, g_ref, layer_ref, hi_ref, lo_ref, tw_ref, r_ref, o_ref, line, v_hi, v_lo, l_hi, l_lo, back
):
    cos, sin = tw_ref[0:1, :], tw_ref[1:2, :]
    for group in range(4):
        parts = [g_ref[:, 4 * group + i].reshape(PLANES, 128) for i in range(4)]
        for q, x in enumerate(exchange(parts)):
            line[q // 2, q % 2, :, 128 * group : 128 * (group + 1)] = x
    for ky in (0, 1):
        first = [line[c, ky, :, :HALF] for c in (0, 1)]
        second = [line[c, ky, :, HALF:] for c in (0, 1)]
        odd = [first[c] - second[c] for c in (0, 1)]
        turned = (odd[0] * cos + odd[1] * sin, odd[1] * cos - odd[0] * sin)
        for c in (0, 1):
            rows = slice(PLANES * c, PLANES * (c + 1))
            v_hi[2 * ky, rows], v_lo[2 * ky, rows] = split(first[c] + second[c])
            v_hi[2 * ky + 1, rows], v_lo[2 * ky + 1, rows] = split(turned[c])

    depth = lax.broadcasted_iota(jnp.int32, (HALF, PLANES), 1).astype(F32)
    layer = layer_ref[...]
    rate_here = jnp.zeros((1, PLANES), F32)
    for l in range(LAYERS):
        rate_here = jnp.where(layer == l, rates_ref[l], rate_here)

    def signed(k):
        return jnp.where(k >= HALF, k - 2 * HALF, k).astype(F32) / HALF

    @pl.loop(0, 4)
    def _(g):
        t_hi, t_lo = hi_ref[...], lo_ref[...]
        out = dot3(t_hi, t_lo, v_hi[g], v_lo[g])
        spec_re = out[:HALF, :PLANES] + out[HALF:, PLANES:]
        spec_im = out[:HALF, PLANES:] - out[HALF:, :PLANES]
        kx = 2 * lax.broadcasted_iota(jnp.int32, (HALF, PLANES), 0) + g % 2
        freq_y = signed(jnp.full((HALF, PLANES), 2 * ky_ref[0] + g // 2, jnp.int32))
        steep = jnp.sqrt(1.0 + signed(kx) ** 2 + freq_y**2)
        scaled = steep * depth
        for l in range(LAYERS):
            angle = scaled * (rates_ref[l] / (2 * PLANES))
            half = jnp.exp(-angle)
            factors = (jnp.exp(2.0 * angle), half * half, half)
            for t, factor in enumerate(factors):
                for c, x in enumerate((spec_re, spec_im)):
                    at = 2 * PLANES * l + PLANES * c
                    l_hi[t, :, at : at + PLANES], l_lo[t, :, at : at + PLANES] = split(x * factor)
        angle = scaled * (rate_here / (2 * PLANES))
        half = jnp.exp(-angle)
        factors = (half * half, jnp.exp(2.0 * angle), half)
        mixed = jnp.zeros((HALF, 2 * PLANES), F32)
        for t in range(3):
            sums = dot3(l_hi[t], l_lo[t], r_ref[2 * t], r_ref[2 * t + 1])
            mixed = mixed + sums * jnp.concatenate([factors[t], factors[t]], 1)
        m_hi, m_lo = split(jnp.transpose(mixed))
        inv = dot3(m_hi, m_lo, t_hi, t_lo)
        back[g, 0] = inv[:PLANES, :HALF] - inv[PLANES:, HALF:]
        back[g, 1] = inv[:PLANES, HALF:] + inv[PLANES:, :HALF]

    for ky in (0, 1):
        even = [back[2 * ky, c] for c in (0, 1)]
        odd = [back[2 * ky + 1, c] for c in (0, 1)]
        turned = (odd[0] * cos - odd[1] * sin, odd[0] * sin + odd[1] * cos)
        for c in (0, 1):
            line[c, ky, :, :HALF] = even[c] + turned[c]
            line[c, ky, :, HALF:] = even[c] - turned[c]
    for group in range(4):
        parts = [line[q // 2, q % 2, :, 128 * group : 128 * (group + 1)] for q in range(4)]
        for i, x in enumerate(exchange(parts)):
            o_ref[:, 4 * group + i] = x.reshape(PLANES // 8, 8, 128)


def inverse_y_kernel(g_ref, contrast_ref, hi_ref, lo_ref, tw_ref, o_ref):
    cos, sin = tw_ref[0:1, :], tw_ref[1:2, :]
    t_hi, t_lo = hi_ref[...], lo_ref[...]
    planes = contrast_ref.shape[0]
    scale = 1.0 / (4 * HALF * HALF)
    for pair in range(planes // 2):
        both = [jnp.transpose(g_ref[pl.ds(2 * pair + k, HALF, stride=8), :]) for k in (0, 1)]
        m_hi, m_lo = split(jnp.concatenate(both, 0))
        out = dot3(m_hi, m_lo, t_hi, t_lo)
        for k in (0, 1):
            real, imag = out[128 * k : 128 * k + 64], out[128 * k + 64 : 128 * (k + 1)]
            re = real[:, :HALF] - imag[:, HALF:]
            im = real[:, HALF:] + imag[:, :HALF]
            turned = (re[32:] * cos - im[32:] * sin, re[32:] * sin + im[32:] * cos)
            z = 2 * pair + k
            for c, even in enumerate((re[:32], im[:32])):
                o_ref[c, z, :, :HALF] = (even + turned[c]) * (contrast_ref[z, :, :HALF] * scale)
                o_ref[c, z, :, HALF:] = (even - turned[c]) * (contrast_ref[z, :, HALF:] * scale)


def vmem(count):
    return [pl.BlockSpec(memory_space=pltpu.VMEM)] * count


def call(kernel, out_shape, operands, flops, scalars=0, scratch=(), limit=32):
    return pl.pallas_call(
        kernel,
        out_shape=out_shape,
        in_specs=[pl.BlockSpec(memory_space=pltpu.SMEM)] * scalars + vmem(len(operands) - scalars),
        out_specs=pl.BlockSpec(memory_space=pltpu.VMEM),
        scratch_shapes=list(scratch),
        compiler_params=pltpu.CompilerParams(vmem_limit_bytes=limit * MIB),
        cost_estimate=pl.CostEstimate(flops=flops, bytes_accessed=4 * MIB, transcendentals=0),
    )(*operands)


def body(wave_field, contrast, layer_of_plane, toeplitz_table, hankel_table, layer_rates):
    t_hi, t_lo, turn = dft_tables()
    t_hi, t_lo, turn = jnp.asarray(t_hi), jnp.asarray(t_lo), jnp.asarray(turn)
    dft = (t_hi, t_lo, turn)
    layer_row = layer_of_plane.reshape(1, PLANES)
    toeplitz = jnp.pad(toeplitz_table[:, :, ::-1], ((0, 0), (0, 0), (0, 1)))
    hankel = jnp.pad(hankel_table, ((0, 0), (0, 0), (0, 1)))
    ky_pair = (lax.axis_index("lay") * lax.axis_size("lat") + lax.axis_index("lat")).reshape(1)

    tiles = jax.ShapeDtypeStruct((2 * HALF * 4, 128), F32)
    sent = call(forward_y_kernel, tiles, (wave_field, *dft), 6 * 2**27)
    mixers = call(
        tables_kernel,
        jax.ShapeDtypeStruct((6, 2 * PLANES, LAYERS * 2 * PLANES), BF16),
        (layer_row, toeplitz, hankel),
        2**28,
    )
    lines = lax.all_to_all(sent.reshape(HALF, 8, 128), AXES, 0, 0, tiled=True)
    lines = call(
        middle_kernel,
        jax.ShapeDtypeStruct((16, 16, 8, 128), F32),
        (layer_rates, ky_pair, lines.reshape(16, 16, 8, 128), layer_row, *dft, mixers),
        2**32,
        scalars=2,
        scratch=(
            pltpu.VMEM((2, 2, PLANES, 2 * HALF), F32),
            pltpu.VMEM((4, 2 * PLANES, HALF), BF16),
            pltpu.VMEM((4, 2 * PLANES, HALF), BF16),
            pltpu.VMEM((3, HALF, LAYERS * 2 * PLANES), BF16),
            pltpu.VMEM((3, HALF, LAYERS * 2 * PLANES), BF16),
            pltpu.VMEM((4, 2, PLANES, HALF), F32),
        ),
        limit=40,
    )
    lines = lax.all_to_all(lines.reshape(HALF, 8, 128), AXES, 0, 0, tiled=True)
    return call(
        inverse_y_kernel,
        jax.ShapeDtypeStruct(wave_field.shape, F32),
        (lines.reshape(2 * HALF * 4, 128), contrast, *dft),
        6 * 2**27,
    )


def solution(mesh):
    return jax.shard_map(
        body,
        mesh=mesh,
        in_specs=(P(None, "lay", "lat", None), P("lay", "lat", None), P(), P(), P(), P()),
        out_specs=P(None, "lay", "lat", None),
        check_vma=False,
    )
```

profile of v0, /device:TPU:1, one launch (start us, length us, event | category | flops | bytes accessed | tf_op | source)
XLA Modules:
  0.0 116.1 jit_solution(18214808732802753172)
XLA Ops:
  0.0 0.0 copy-start.8
  0.0 0.0 copy-start.3
  0.0 1.0 copy-done.3
  1.0 0.0 copy-start.5
  1.0 0.9 copy-done.5
  1.9 0.0 copy-start.7
  1.9 0.7 copy-done.7
  2.6 0.0 copy-start.11
  2.6 1.2 %copy-done.11 = f32[2,8,32,512]{3,2,1,0:T(8,128)S(1)} copy-done((f32[2,8,32,512]{3,2,1,0:T(8,128)S(1)}, f32[2,8,32,512]{3,2,1,0:T(8,128)}, u32[]{:S(2)}) %copy-start.11) | copy-done | bytes 1048600
  3.8 0.0 copy-start.4
  3.8 0.0 copy-start.6
  3.8 0.0 copy-start.10
  3.8 0.0 copy-start.12
  3.8 2.2 %shard_map.91 = f32[2048,128]{1,0:T(8,128)} custom-call(f32[2,8,32,512]{3,2,1,0:T(8,128)S(1)} %copy-done.11, bf16[512,256]{1,0:T(8,128)(2,1)S(1)} %copy-done.5, bf16[512,256]{1,0:T(8,128)(2,1)S(1)} %copy-done.3, f32[2,256]{1,0:T(2,128)S(1)} %copy-done.7), custom_call_target="tpu_custom_call" | custom-call | flops 805306368 | bytes 4194304 | tf_op jit(solution)/shard_map/pallas_call | solution.py:213
  6.0 15.7 %all-to-all-start = ((f32[256,8,128]{2,1,0:T(8,128)}), f32[256,8,128]{2,1,0:T(8,128)S(1)}, u32[]{:S(2)}, u32[]{:S(2)}) async-start(f32[256,8,128]{2,1,0:T(8,128)} %bitcast.1), calls=%async_computation | async-start | bytes 2097152 | tf_op jit(solution)/shard_map/all_to_all | solution.py:241
  21.7 0.8 reverse
  22.5 0.1 slice
  22.6 0.7 pad.8.han_ref
  23.3 0.0 copy-start.9
  23.3 0.7 copy-done.9
  24.0 2.8 %shard_map.92.r_ref = bf16[6,256,2048]{2,1,0:T(8,128)(2,1)S(1)} custom-call(s32[1,128]{1,0:T(1,128)S(1)} %bitcast.10, f32[2,8,256]{2,1,0:T(8,128)S(1)} %pad.7.toe_ref, f32[2,8,256]{2,1,0:T(8,128)S(1)} %pad.8.han_ref), custom_call_target="tpu_custom_call" | custom-call | flops 268435456 | bytes 4194304 | tf_op jit(solution)/shard_map/pallas_call | solution.py:213
  26.8 0.0 copy-start
  26.8 2.6 %copy-done = bf16[6,256,2048]{2,1,0:T(8,128)(2,1)} copy-done((bf16[6,256,2048]{2,1,0:T(8,128)(2,1)}, bf16[6,256,2048]{2,1,0:T(8,128)(2,1)S(1)}, u32[]{:S(2)}) %copy-start) | copy-done | bytes 6291480
  29.4 23.9 %all-to-all-done = f32[256,8,128]{2,1,0:T(8,128)S(1)} async-done(((f32[256,8,128]{2,1,0:T(8,128)}), f32[256,8,128]{2,1,0:T(8,128)S(1)}, u32[]{:S(2)}, u32[]{:S(2)}) %all-to-all-start) | async-done | bytes 1048608 | tf_op jit(solution)/shard_map/all_to_all | solution.py:241
  53.3 0.0 copy-done.8
  53.3 0.0 copy-done.4
  53.3 0.0 copy-done.6
  53.3 0.0 copy-done.10
  53.3 0.0 copy-done.12
  53.3 0.0 copy-start.1
  53.4 2.8 %copy-done.1 = bf16[6,256,2048]{2,1,0:T(8,128)(2,1)S(1)} copy-done((bf16[6,256,2048]{2,1,0:T(8,128)(2,1)S(1)}, bf16[6,256,2048]{2,1,0:T(8,128)(2,1)}, u32[]{:S(2)}) %copy-start.1) | copy-done | bytes 6291480
  56.1 0.0 copy-start.2
  56.1 21.0 %shard_map.93 = f32[16,16,8,128]{3,2,1,0:T(8,128)S(1)} custom-call(f32[8]{0:T(128)S(1)} %copy-done.12, s32[1]{0:T(128)} %bitcast.ky_ref, f32[16,16,8,128]{3,2,1,0:T(8,128)S(1)} %bitcast.8, s32[1,128]{1,0:T(1,128)S(1)} %bitcast.11, bf16[512,256]{1,0:T(8,128)(2,1)S(1)} %copy-done.6, bf16[512,256]{1,0:T(8,128)(2,1)S(1)} %copy-done.4, f32[2,256]{1,0:T(2,128)S(1)} %copy-done.8, ...), custom_call_target="tpu_custom_call" | custom-call | flops 4294967296 | bytes 4194304 | tf_op jit(solution)/shard_map/pallas_call | solution.py:213
  77.2 36.8 %all_to_all.10 = f32[256,8,128]{2,1,0:T(8,128)S(1)} all-to-all(f32[256,8,128]{2,1,0:T(8,128)S(1)} %bitcast.9), channel_id=1, replica_groups=mesh['lat'=16,'lay'=16] {'lay','lat'}, dimensions={0} | all-to-all | bytes 2097152 | tf_op jit(solution)/shard_map/all_to_all | solution.py:258
  113.9 0.0 copy-done.2
  113.9 2.2 %shard_map.94 = f32[2,8,32,512]{3,2,1,0:T(8,128)} custom-call(f32[2048,128]{1,0:T(8,128)S(1)} %bitcast.7, f32[8,32,512]{2,1,0:T(8,128)S(1)} %copy-done.2, bf16[512,256]{1,0:T(8,128)(2,1)S(1)} %copy-done.6, bf16[512,256]{1,0:T(8,128)(2,1)S(1)} %copy-done.4, f32[2,256]{1,0:T(2,128)S(1)} %copy-done.8), custom_call_target="tpu_custom_call" | custom-call | flops 805306368 | bytes 4194304 | tf_op jit(solution)/shard_map/pallas_call | solution.py:213
  (1 shorter events, 0.0 us)
Async XLA Ops:
  0.0 53.3 %copy-start.8 = (f32[2,256]{1,0:T(2,128)S(1)}, f32[2,256]{1,0:T(2,128)}, u32[]{:S(2)}) copy-start(f32[2,256]{1,0:T(2,128)} %constant.20.clone.tw_ref) | copy-start | bytes 6148
  0.0 1.0 copy-start.3
  1.0 0.9 copy-start.5
  1.9 0.7 copy-start.7
  2.6 1.2 %copy-start.11 = (f32[2,8,32,512]{3,2,1,0:T(8,128)S(1)}, f32[2,8,32,512]{3,2,1,0:T(8,128)}, u32[]{:S(2)}) copy-start(f32[2,8,32,512]{3,2,1,0:T(8,128)} %w_ref.1) | copy-start | bytes 3145732
  3.8 49.5 %copy-start.4 = (bf16[512,256]{1,0:T(8,128)(2,1)S(1)}, bf16[512,256]{1,0:T(8,128)(2,1)}, u32[]{:S(2)}) copy-start(bf16[512,256]{1,0:T(8,128)(2,1)} %constant.19.clone.lo_ref) | copy-start | bytes 786436
  3.8 49.5 %copy-start.6 = (bf16[512,256]{1,0:T(8,128)(2,1)S(1)}, bf16[512,256]{1,0:T(8,128)(2,1)}, u32[]{:S(2)}) copy-start(bf16[512,256]{1,0:T(8,128)(2,1)} %constant.18.clone.hi_ref) | copy-start | bytes 786436
  3.8 49.5 %copy-start.10 = (s32[128]{0:T(128)S(1)}, s32[128]{0:T(128)}, u32[]{:S(2)}) copy-start(s32[128]{0:T(128)} %param.11) | copy-start | bytes 1540
  3.8 49.5 %copy-start.12 = (f32[8]{0:T(128)S(1)}, f32[8]{0:T(128)}, u32[]{:S(2)}) copy-start(f32[8]{0:T(128)} %rates_ref.1) | copy-start | bytes 100
  6.0 47.3 %all-to-all-start = ((f32[256,8,128]{2,1,0:T(8,128)}), f32[256,8,128]{2,1,0:T(8,128)S(1)}, u32[]{:S(2)}, u32[]{:S(2)}) async-start(f32[256,8,128]{2,1,0:T(8,128)} %bitcast.1), calls=%async_computation | async-start | bytes 2097152 | tf_op jit(solution)/shard_map/all_to_all | solution.py:241
  23.3 0.7 copy-start.9
  26.8 2.6 %copy-start = (bf16[6,256,2048]{2,1,0:T(8,128)(2,1)}, bf16[6,256,2048]{2,1,0:T(8,128)(2,1)S(1)}, u32[]{:S(2)}) copy-start(bf16[6,256,2048]{2,1,0:T(8,128)(2,1)S(1)} %shard_map.92.r_ref) | copy-start | bytes 18874372
  53.3 2.8 %copy-start.1 = (bf16[6,256,2048]{2,1,0:T(8,128)(2,1)S(1)}, bf16[6,256,2048]{2,1,0:T(8,128)(2,1)}, u32[]{:S(2)}) copy-start(bf16[6,256,2048]{2,1,0:T(8,128)(2,1)} %copy-done) | copy-start | bytes 18874372
  56.1 57.8 %copy-start.2 = (f32[8,32,512]{2,1,0:T(8,128)S(1)}, f32[8,32,512]{2,1,0:T(8,128)}, u32[]{:S(2)}) copy-start(f32[8,32,512]{2,1,0:T(8,128)} %contrast_ref.1) | copy-start | bytes 1572868
where the time goes:
time: 117 us; the launch traced here: 116 us
  blocking collectives  36.8 us (31%)
  Pallas kernels  28.1 us (24%)
  waiting for transfers between devices  23.9 us (20%)
  starting transfers between devices  15.7 us (13%)
  local copies, waits for them, and re-layouts  11.6 us (10%)
    all_to_all x1, blocking collectives, body(): lines = lax.all_to_all(lines.reshape(HALF, 8, 128), AXES, 0, 0, tiled=True)  36.8 us
    pallas_call x4, Pallas kernels, call(): pl.pallas_call(kernel, out_shape=out_shape, in_specs=[pl.BlockSpec(memory...  28.1 us
    all_to_all x1, waiting for transfers between devices, body(): lines = lax.all_to_all(sent.reshape(HALF, 8, 128), AXES, 0, 0, tiled=True)  23.9 us
    all_to_all x1, starting transfers between devices, body(): lines = lax.all_to_all(sent.reshape(HALF, 8, 128), AXES, 0, 0, tiled=True)  15.7 us
    unnamed x28, local copies, waits for them, and re-layouts  10.8 us
  transfers between devices with their start and end apart: 1, of which 1 were waited for; matrix products, arithmetic and copies ran while one was open for 1% of the time, Pallas kernels for 2%

commit v1 on v0

--- a/solution.py
+++ b/solution.py
@@ -16,6 +16,7 @@
 HALF = 256
 PLANES = 128
 LAYERS = 8
+WINDOW = 40
 MIB = 1 << 20
 
 
@@ -41,6 +42,14 @@
 
 def dot_nt(a, b):
     return lax.dot_general(a, b, (((1,), (1,)), ((), ())), preferred_element_type=F32)
+
+
+def window_of(p):
+    return pl.multiple_of((p >> 3) << 3, 8)
+
+
+def dot_nn(a, b):
+    return jnp.dot(a, b, preferred_element_type=F32)
 
 
 def dot3(a_hi, a_lo, b_hi, b_lo):
@@ -70,37 +79,45 @@
             o_ref[pl.ds(2 * pair + k, HALF, stride=8), :] = with_cos + jnp.where(lane < 64, with_sin, -with_sin)
 
 
-def tables_kernel(layer_ref, toe_ref, han_ref, r_ref):
-    layer_rows = jnp.transpose(jnp.broadcast_to(layer_ref[...].astype(F32), (PLANES, PLANES)))
-    wide = jnp.concatenate([layer_rows, layer_rows], 1)
+def tables_kernel(start_ref, toe_ref, han_ref, w_ref, own_ref, plane_rows):
     row = lax.broadcasted_iota(jnp.int32, (PLANES, 2 * PLANES), 0)
 
     def spread(ref, c, amount):
         x = jnp.zeros((PLANES, 2 * PLANES), F32)
         for l in range(LAYERS):
-            x = jnp.where(wide == float(l), ref[c, l : l + 1, :], x)
+            x = jnp.where(row >= start_ref[l], ref[c, l : l + 1, :], x)
         for bit in range(7):
             moved = pltpu.roll(x, 2 * PLANES - (1 << bit), 1)
             x = jnp.where(((amount >> bit) & 1) == 1, moved, x)
         return x[:, :PLANES]
 
-    toe = [spread(toe_ref, c, PLANES - 1 - row) for c in (0, 1)]
-    han = [spread(han_ref, c, row) for c in (0, 1)]
+    def blocks(re, im):
+        return jnp.concatenate([jnp.concatenate([re, -im], 1), jnp.concatenate([im, re], 1)], 0)
+
+    plane_rows[:, PLANES:] = jnp.zeros((4, WINDOW, PLANES), F32)
+    for c in (0, 1):
+        plane_rows[c, :PLANES] = spread(toe_ref, c, PLANES - 1 - row)
+        plane_rows[2 + c, :PLANES] = spread(han_ref, c, row)
     z = lax.broadcasted_iota(jnp.int32, (PLANES, PLANES), 0)
     s = lax.broadcasted_iota(jnp.int32, (PLANES, PLANES), 1)
-    low = [jnp.where(s <= z, x, 0.0) for x in toe]
-    high = [jnp.where(s > z, x, 0.0) for x in toe]
-    for t, (re, im) in enumerate((low, high, han)):
-        for out_part, blocks in enumerate(((re, -im), (im, re))):
-            for in_part, block in enumerate(blocks):
-                hi = block.astype(BF16).astype(F32)
-                lo = block - hi
-                for l in range(LAYERS):
-                    here = layer_rows == float(l)
-                    rows = slice(PLANES * out_part, PLANES * (out_part + 1))
-                    at = 2 * PLANES * l + PLANES * in_part
-                    r_ref[2 * t, rows, at : at + PLANES] = jnp.where(here, hi, 0.0).astype(BF16)
-                    r_ref[2 * t + 1, rows, at : at + PLANES] = jnp.where(here, lo, 0.0).astype(BF16)
+    first = jnp.zeros((PLANES, PLANES), jnp.int32)
+    for l in range(LAYERS):
+        first = jnp.where(z >= start_ref[l], start_ref[l], first)
+    inside = (s >= first) & (s <= z)
+    hi, lo = split(blocks(*(jnp.where(inside, plane_rows[c, :PLANES], 0.0) for c in (0, 1))))
+    own_ref[: 2 * PLANES], own_ref[2 * PLANES :] = hi, lo
+    j = lax.broadcasted_iota(jnp.int32, (WINDOW, PLANES), 0)
+    s = lax.broadcasted_iota(jnp.int32, (WINDOW, PLANES), 1)
+    for l in range(LAYERS):
+        p = start_ref[l]
+        q = window_of(p)
+        re, im, hre, him = (plane_rows[i, pl.ds(q, WINDOW), :] for i in range(4))
+        later = jnp.maximum(q + j, p - 1)
+        before = blocks(jnp.where(s < p, re, 0.0), jnp.where(s < p, im, 0.0))
+        after = blocks(jnp.where(s > later, re, 0.0), jnp.where(s > later, im, 0.0))
+        hi, lo = split(jnp.concatenate([before, after], 0))
+        w_ref[l, : 4 * WINDOW], w_ref[l, 4 * WINDOW : 8 * WINDOW] = hi, lo
+        w_ref[l, 8 * WINDOW : 10 * WINDOW], w_ref[l, 10 * WINDOW :] = split(blocks(hre, him))
 
 
 def exchange(parts):
@@ -116,7 +133,7 @@
 
 
 def middle_kernel(
-    rates_ref, ky_ref, g_ref, layer_ref, hi_ref, lo_ref, tw_ref, r_ref, o_ref, line, v_hi, v_lo, l_hi, l_lo, back
+    rates_ref, start_ref, ky_ref, g_ref, hi_ref, lo_ref, tw_ref, w_ref, own_ref, o_ref, line, v_hi, v_lo, own, mixed, back
 ):
     cos, sin = tw_ref[0:1, :], tw_ref[1:2, :]
     for group in range(4):
@@ -133,11 +150,13 @@
             v_hi[2 * ky, rows], v_lo[2 * ky, rows] = split(first[c] + second[c])
             v_hi[2 * ky + 1, rows], v_lo[2 * ky + 1, rows] = split(turned[c])
 
-    depth = lax.broadcasted_iota(jnp.int32, (HALF, PLANES), 1).astype(F32)
-    layer = layer_ref[...]
-    rate_here = jnp.zeros((1, PLANES), F32)
+    own[:, PLANES:] = jnp.zeros((2, WINDOW, HALF), F32)
+    plane = lax.broadcasted_iota(jnp.int32, (PLANES, HALF), 0).astype(F32)
+    own_depth = jnp.zeros((PLANES, HALF), F32)
     for l in range(LAYERS):
-        rate_here = jnp.where(layer == l, rates_ref[l], rate_here)
+        p = start_ref[l].astype(F32)
+        own_depth = jnp.where(plane >= p, (plane - p) * (rates_ref[l] / PLANES), own_depth)
+    window = lax.broadcasted_iota(jnp.int32, (WINDOW, HALF), 0).astype(F32)
 
     def signed(k):
         return jnp.where(k >= HALF, k - 2 * HALF, k).astype(F32) / HALF
@@ -145,29 +164,44 @@
     @pl.loop(0, 4)
     def _(g):
         t_hi, t_lo = hi_ref[...], lo_ref[...]
-        out = dot3(t_hi, t_lo, v_hi[g], v_lo[g])
-        spec_re = out[:HALF, :PLANES] + out[HALF:, PLANES:]
-        spec_im = out[:HALF, PLANES:] - out[HALF:, :PLANES]
-        kx = 2 * lax.broadcasted_iota(jnp.int32, (HALF, PLANES), 0) + g % 2
-        freq_y = signed(jnp.full((HALF, PLANES), 2 * ky_ref[0] + g // 2, jnp.int32))
+        out = dot3(v_hi[g], v_lo[g], t_hi, t_lo)
+        spec_re = out[:PLANES, :HALF] + out[PLANES:, HALF:]
+        spec_im = out[PLANES:, :HALF] - out[:PLANES, HALF:]
+        kx = 2 * lax.broadcasted_iota(jnp.int32, (1, HALF), 1) + g % 2
+        freq_y = signed(jnp.full((1, HALF), 2 * ky_ref[0] + g // 2, jnp.int32))
         steep = jnp.sqrt(1.0 + signed(kx) ** 2 + freq_y**2)
-        scaled = steep * depth
+
+        def weighted(factor):
+            return split(jnp.concatenate([spec_re * factor, spec_im * factor], 0))
+
+        x_hi, x_lo = weighted(jnp.exp(own_depth * steep))
+        sums = dot_nn(own_ref[...], x_hi)
+        sums = sums[: 2 * PLANES] + sums[2 * PLANES :] + dot_nn(own_ref[: 2 * PLANES], x_lo)
+        own[0, :PLANES], own[1, :PLANES] = sums[:PLANES], sums[PLANES:]
         for l in range(LAYERS):
-            angle = scaled * (rates_ref[l] / (2 * PLANES))
-            half = jnp.exp(-angle)
-            factors = (jnp.exp(2.0 * angle), half * half, half)
-            for t, factor in enumerate(factors):
-                for c, x in enumerate((spec_re, spec_im)):
-                    at = 2 * PLANES * l + PLANES * c
-                    l_hi[t, :, at : at + PLANES], l_lo[t, :, at : at + PLANES] = split(x * factor)
-        angle = scaled * (rate_here / (2 * PLANES))
-        half = jnp.exp(-angle)
-        factors = (half * half, jnp.exp(2.0 * angle), half)
-        mixed = jnp.zeros((HALF, 2 * PLANES), F32)
-        for t in range(3):
-            sums = dot3(l_hi[t], l_lo[t], r_ref[2 * t], r_ref[2 * t + 1])
-            mixed = mixed + sums * jnp.concatenate([factors[t], factors[t]], 1)
-        m_hi, m_lo = split(jnp.transpose(mixed))
+            p = start_ref[l]
+            depth = p.astype(F32)
+            rate = rates_ref[l] / PLANES
+            x_hi, x_lo = weighted(jnp.exp((jnp.abs(plane - depth) * -rate) * steep))
+            direct = dot_nn(w_ref[l, : 8 * WINDOW], x_hi)
+            direct = direct[: 4 * WINDOW] + direct[4 * WINDOW :] + dot_nn(w_ref[l, : 4 * WINDOW], x_lo)
+            x_hi, x_lo = weighted(jnp.exp((plane * (-0.5 * rate)) * steep))
+            reflected = dot_nn(w_ref[l, 8 * WINDOW :], x_hi)
+            reflected = reflected[: 2 * WINDOW] + reflected[2 * WINDOW :] + dot_nn(w_ref[l, 8 * WINDOW : 10 * WINDOW], x_lo)
+            q = window_of(p)
+            there = window + q.astype(F32)
+            angle = (there - depth) * (rate * steep)
+            fade, rise = jnp.exp(-angle), jnp.exp(angle)
+            far = jnp.exp(there * (-0.5 * rate * steep))
+            for c in (0, 1):
+                rows = slice(WINDOW * c, WINDOW * (c + 1))
+                near = direct[rows] + own[c, pl.ds(q, WINDOW), :]
+                after = direct[2 * WINDOW + WINDOW * c : 3 * WINDOW + WINDOW * c]
+                sums = near * fade + after * rise + reflected[rows] * far
+                kept = mixed[c, pl.ds(q, 8), :]
+                mixed[c, pl.ds(q, 8), :] = jnp.where(there[:8] >= depth, sums[:8], kept)
+                mixed[c, pl.ds(pl.multiple_of(q + 8, 8), WINDOW - 8), :] = sums[8:]
+        m_hi, m_lo = split(jnp.concatenate([mixed[0, :PLANES], mixed[1, :PLANES]], 0))
         inv = dot3(m_hi, m_lo, t_hi, t_lo)
         back[g, 0] = inv[:PLANES, :HALF] - inv[PLANES:, HALF:]
         back[g, 1] = inv[:PLANES, HALF:] + inv[PLANES:, :HALF]
@@ -209,12 +243,12 @@
     return [pl.BlockSpec(memory_space=pltpu.VMEM)] * count
 
 
-def call(kernel, out_shape, operands, flops, scalars=0, scratch=(), limit=32):
+def call(kernel, out_shape, operands, flops, scalars=0, scratch=(), limit=16):
     return pl.pallas_call(
         kernel,
         out_shape=out_shape,
         in_specs=[pl.BlockSpec(memory_space=pltpu.SMEM)] * scalars + vmem(len(operands) - scalars),
-        out_specs=pl.BlockSpec(memory_space=pltpu.VMEM),
+        out_specs=jax.tree.map(lambda _: pl.BlockSpec(memory_space=pltpu.VMEM), out_shape),
         scratch_shapes=list(scratch),
         compiler_params=pltpu.CompilerParams(vmem_limit_bytes=limit * MIB),
         cost_estimate=pl.CostEstimate(flops=flops, bytes_accessed=4 * MIB, transcendentals=0),
@@ -225,35 +259,42 @@
     t_hi, t_lo, turn = dft_tables()
     t_hi, t_lo, turn = jnp.asarray(t_hi), jnp.asarray(t_lo), jnp.asarray(turn)
     dft = (t_hi, t_lo, turn)
-    layer_row = layer_of_plane.reshape(1, PLANES)
+    ids = jnp.arange(LAYERS, dtype=jnp.int32)
+    starts = jnp.sum((layer_of_plane[None, :] < ids[:, None]).astype(jnp.int32), axis=1)
     toeplitz = jnp.pad(toeplitz_table[:, :, ::-1], ((0, 0), (0, 0), (0, 1)))
     hankel = jnp.pad(hankel_table, ((0, 0), (0, 0), (0, 1)))
     ky_pair = (lax.axis_index("lay") * lax.axis_size("lat") + lax.axis_index("lat")).reshape(1)
 
     tiles = jax.ShapeDtypeStruct((2 * HALF * 4, 128), F32)
     sent = call(forward_y_kernel, tiles, (wave_field, *dft), 6 * 2**27)
-    mixers = call(
+    window_mix, own_mix = call(
         tables_kernel,
-        jax.ShapeDtypeStruct((6, 2 * PLANES, LAYERS * 2 * PLANES), BF16),
-        (layer_row, toeplitz, hankel),
+        (
+            jax.ShapeDtypeStruct((LAYERS, 12 * WINDOW, 2 * PLANES), BF16),
+            jax.ShapeDtypeStruct((4 * PLANES, 2 * PLANES), BF16),
+        ),
+        (starts, toeplitz, hankel),
         2**28,
+        scalars=1,
+        scratch=(pltpu.VMEM((4, PLANES + WINDOW, PLANES), F32),),
+        limit=12,
     )
     lines = lax.all_to_all(sent.reshape(HALF, 8, 128), AXES, 0, 0, tiled=True)
     lines = call(
         middle_kernel,
         jax.ShapeDtypeStruct((16, 16, 8, 128), F32),
-        (layer_rates, ky_pair, lines.reshape(16, 16, 8, 128), layer_row, *dft, mixers),
+        (layer_rates, starts, ky_pair, lines.reshape(16, 16, 8, 128), *dft, window_mix, own_mix),
         2**32,
-        scalars=2,
+        scalars=3,
         scratch=(
             pltpu.VMEM((2, 2, PLANES, 2 * HALF), F32),
             pltpu.VMEM((4, 2 * PLANES, HALF), BF16),
             pltpu.VMEM((4, 2 * PLANES, HALF), BF16),
-            pltpu.VMEM((3, HALF, LAYERS * 2 * PLANES), BF16),
-            pltpu.VMEM((3, HALF, LAYERS * 2 * PLANES), BF16),
+            pltpu.VMEM((2, PLANES + WINDOW, HALF), F32),
+            pltpu.VMEM((2, PLANES + WINDOW, HALF), F32),
             pltpu.VMEM((4, 2, PLANES, HALF), F32),
         ),
-        limit=40,
+        limit=20,
     )
     lines = lax.all_to_all(lines.reshape(HALF, 8, 128), AXES, 0, 0, tiled=True)
     return call(

time: 117 us -> 108 us (0.923)
  Pallas kernels: 28.1 us -> 20.8 us
  local copies, waits for them, and re-layouts: 11.6 us -> 6.94 us
  waiting for transfers between devices: 23.9 us -> 26.9 us
    pallas_call x4, Pallas kernels: 28.1 us -> 20.8 us  [call(): pl.pallas_call(kernel, out_shape=out_shape, in_specs=[pl.BlockSpec(memory...]
    unnamed x28 -> x30, local copies, waits for them, and re-layouts: 10.8 us -> 6.92 us
    all_to_all x1, waiting for transfers between devices: 23.9 us -> 26.9 us  [body(): lines = lax.all_to_all(sent.reshape(HALF, 8, 128), AXES, 0, 0, tiled=True)]
  transfers between devices with their start and end apart: 1 -> 1, of which waited for: 1 -> 1; matrix products, arithmetic and copies ran while one was open for 1% -> 0% of each run, Pallas kernels for 2% -> 3%
where the time goes in v1:
time: 108 us; the launch traced here: 107 us
  blocking collectives  36.8 us (34%)
  waiting for transfers between devices  26.9 us (25%)
  Pallas kernels  20.8 us (19%)
  starting transfers between devices  15.7 us (15%)
  local copies, waits for them, and re-layouts  6.94 us (6%)
    all_to_all x1, blocking collectives, body(): lines = lax.all_to_all(lines.reshape(HALF, 8, 128), AXES, 0, 0, tiled=True)  36.8 us
    all_to_all x1, waiting for transfers between devices, body(): lines = lax.all_to_all(sent.reshape(HALF, 8, 128), AXES, 0, 0, tiled=True)  26.9 us
    pallas_call x4, Pallas kernels, call(): pl.pallas_call(kernel, out_shape=out_shape, in_specs=[pl.BlockSpec(memory...  20.8 us
    all_to_all x1, starting transfers between devices, body(): lines = lax.all_to_all(sent.reshape(HALF, 8, 128), AXES, 0, 0, tiled=True)  15.7 us
    unnamed x30, local copies, waits for them, and re-layouts  6.92 us
  transfers between devices with their start and end apart: 1, of which 1 were waited for; matrix products, arithmetic and copies ran while one was open for 0% of the time, Pallas kernels for 3%

profile of v1, /device:TPU:1, one launch (start us, length us, event | category | flops | bytes accessed | tf_op | source)
XLA Modules:
  0.0 107.3 jit_solution(10330971199620212366)
XLA Ops:
  0.0 0.0 copy-start.1
  0.0 0.9 copy-done.1
  1.0 0.0 copy-start.3
  1.0 0.9 copy-done.3
  1.9 0.0 copy-start.5
  1.9 0.7 copy-done.5
  2.6 0.0 copy-start.7
  2.6 1.2 %copy-done.7 = f32[2,8,32,512]{3,2,1,0:T(8,128)S(1)} copy-done((f32[2,8,32,512]{3,2,1,0:T(8,128)S(1)}, f32[2,8,32,512]{3,2,1,0:T(8,128)}, u32[]{:S(2)}) %copy-start.7) | copy-done | bytes 1048600
  3.8 0.0 copy-start.11
  3.8 0.0 copy-start.12
  3.8 0.0 copy-start.13
  3.8 2.2 %shard_map.91 = f32[2048,128]{1,0:T(8,128)} custom-call(f32[2,8,32,512]{3,2,1,0:T(8,128)S(1)} %copy-done.7, bf16[512,256]{1,0:T(8,128)(2,1)S(1)} %copy-done.3, bf16[512,256]{1,0:T(8,128)(2,1)S(1)} %copy-done.1, f32[2,256]{1,0:T(2,128)S(1)} %copy-done.5), custom_call_target="tpu_custom_call" | custom-call | flops 805306368 | bytes 4194304 | tf_op jit(solution)/shard_map/pallas_call | solution.py:247
  6.0 0.0 copy-start.2
  6.0 0.0 copy-start.4
  6.0 0.0 copy-start.6
  6.0 0.0 copy-start.8
  6.0 15.7 %all-to-all-start = ((f32[256,8,128]{2,1,0:T(8,128)}), f32[256,8,128]{2,1,0:T(8,128)S(1)}, u32[]{:S(2)}, u32[]{:S(2)}) async-start(f32[256,8,128]{2,1,0:T(8,128)} %bitcast.1), calls=%async_computation | async-start | bytes 2097152 | tf_op jit(solution)/shard_map/all_to_all | solution.py:282
  21.7 0.0 copy-done.11
  21.7 0.2 reverse
  21.8 0.1 slice
  21.9 0.0 copy-done.12
  22.0 0.0 copy-done.13
  22.0 0.1 convert_reduce_fusion.start_ref
  22.1 3.0 %shard_map.92 = (bf16[8,480,256]{2,1,0:T(8,128)(2,1)S(1)}, bf16[512,256]{1,0:T(8,128)(2,1)S(1)}) custom-call(s32[8]{0:T(128)S(1)} %convert_reduce_fusion.start_ref, f32[2,8,256]{2,1,0:T(8,128)S(1)} %pad.7.toe_ref, f32[2,8,256]{2,1,0:T(8,128)S(1)} %pad.8.han_ref), custom_call_target="tpu_custom_call" | custom-call | flops 268435456 | bytes 4194304 | tf_op jit(solution)/shard_map/pallas_call | solution.py:247
  25.1 0.0 copy-start.9
  25.1 1.3 %copy-done.9 = bf16[8,480,256]{2,1,0:T(8,128)(2,1)} copy-done((bf16[8,480,256]{2,1,0:T(8,128)(2,1)}, bf16[8,480,256]{2,1,0:T(8,128)(2,1)S(1)}, u32[]{:S(2)}) %copy-start.9) | copy-done | bytes 1966104
  26.4 26.9 %all-to-all-done = f32[256,8,128]{2,1,0:T(8,128)S(1)} async-done(((f32[256,8,128]{2,1,0:T(8,128)}), f32[256,8,128]{2,1,0:T(8,128)S(1)}, u32[]{:S(2)}, u32[]{:S(2)}) %all-to-all-start) | async-done | bytes 1048608 | tf_op jit(solution)/shard_map/all_to_all | solution.py:282
  53.3 0.0 copy-done.2
  53.3 0.0 copy-done.4
  53.3 0.0 copy-done.6
  53.3 0.0 copy-done.8
  53.3 0.0 copy-start.10
  53.3 1.5 %copy-done.10 = bf16[8,480,256]{2,1,0:T(8,128)(2,1)S(1)} copy-done((bf16[8,480,256]{2,1,0:T(8,128)(2,1)S(1)}, bf16[8,480,256]{2,1,0:T(8,128)(2,1)}, u32[]{:S(2)}) %copy-start.10) | copy-done | bytes 1966104
  54.9 13.5 %shard_map.93 = f32[16,16,8,128]{3,2,1,0:T(8,128)S(1)} custom-call(f32[8]{0:T(128)S(1)} %copy-done.8, s32[8]{0:T(128)S(1)} %convert_reduce_fusion.start_ref, s32[1]{0:T(128)} %bitcast.ky_ref, f32[16,16,8,128]{3,2,1,0:T(8,128)S(1)} %bitcast.7, bf16[512,256]{1,0:T(8,128)(2,1)S(1)} %copy-done.4, bf16[512,256]{1,0:T(8,128)(2,1)S(1)} %copy-done.2, ...), custom_call_target="tpu_custom_call" | custom-call | flops 4294967296 | bytes 4194304 | tf_op jit(solution)/shard_map/pallas_call | solution.py:247
  68.4 0.0 copy-start
  68.4 36.8 %all_to_all.10 = f32[256,8,128]{2,1,0:T(8,128)S(1)} all-to-all(f32[256,8,128]{2,1,0:T(8,128)S(1)} %bitcast.8), channel_id=1, replica_groups=mesh['lat'=16,'lay'=16] {'lay','lat'}, dimensions={0} | all-to-all | bytes 2097152 | tf_op jit(solution)/shard_map/all_to_all | solution.py:299
  105.2 0.0 copy-done
  105.2 2.2 %shard_map.94 = f32[2,8,32,512]{3,2,1,0:T(8,128)} custom-call(f32[2048,128]{1,0:T(8,128)S(1)} %bitcast.6, f32[8,32,512]{2,1,0:T(8,128)S(1)} %copy-done, bf16[512,256]{1,0:T(8,128)(2,1)S(1)} %copy-done.4, bf16[512,256]{1,0:T(8,128)(2,1)S(1)} %copy-done.2, f32[2,256]{1,0:T(2,128)S(1)} %copy-done.6), custom_call_target="tpu_custom_call" | custom-call | flops 805306368 | bytes 4194304 | tf_op jit(solution)/shard_map/pallas_call | solution.py:247
  (2 shorter events, 0.0 us)
Async XLA Ops:
  0.0 0.9 copy-start.1
  1.0 0.9 copy-start.3
  1.9 0.7 copy-start.5
  2.6 1.2 %copy-start.7 = (f32[2,8,32,512]{3,2,1,0:T(8,128)S(1)}, f32[2,8,32,512]{3,2,1,0:T(8,128)}, u32[]{:S(2)}) copy-start(f32[2,8,32,512]{3,2,1,0:T(8,128)} %w_ref.1) | copy-start | bytes 3145732
  3.8 17.9 %copy-start.11 = (f32[2,8,255]{2,1,0:T(8,128)S(1)}, f32[2,8,255]{2,1,0:T(8,128)}, u32[]{:S(2)}) copy-start(f32[2,8,255]{2,1,0:T(8,128)} %param.12) | copy-start | bytes 48964
  3.8 18.1 %copy-start.12 = (f32[2,8,255]{2,1,0:T(8,128)S(1)}, f32[2,8,255]{2,1,0:T(8,128)}, u32[]{:S(2)}) copy-start(f32[2,8,255]{2,1,0:T(8,128)} %param.13) | copy-start | bytes 48964
  3.8 18.1 %copy-start.13 = (s32[128]{0:T(128)S(1)}, s32[128]{0:T(128)}, u32[]{:S(2)}) copy-start(s32[128]{0:T(128)} %param.11) | copy-start | bytes 1540
  6.0 47.3 %copy-start.2 = (bf16[512,256]{1,0:T(8,128)(2,1)S(1)}, bf16[512,256]{1,0:T(8,128)(2,1)}, u32[]{:S(2)}) copy-start(bf16[512,256]{1,0:T(8,128)(2,1)} %constant.20.clone.lo_ref) | copy-start | bytes 786436
  6.0 47.3 %copy-start.4 = (bf16[512,256]{1,0:T(8,128)(2,1)S(1)}, bf16[512,256]{1,0:T(8,128)(2,1)}, u32[]{:S(2)}) copy-start(bf16[512,256]{1,0:T(8,128)(2,1)} %constant.19.clone.hi_ref) | copy-start | bytes 786436
  6.0 47.3 %copy-start.6 = (f32[2,256]{1,0:T(2,128)S(1)}, f32[2,256]{1,0:T(2,128)}, u32[]{:S(2)}) copy-start(f32[2,256]{1,0:T(2,128)} %constant.21.clone.tw_ref) | copy-start | bytes 6148
  6.0 47.3 %copy-start.8 = (f32[8]{0:T(128)S(1)}, f32[8]{0:T(128)}, u32[]{:S(2)}) copy-start(f32[8]{0:T(128)} %rates_ref.1) | copy-start | bytes 100
  6.0 47.3 %all-to-all-start = ((f32[256,8,128]{2,1,0:T(8,128)}), f32[256,8,128]{2,1,0:T(8,128)S(1)}, u32[]{:S(2)}, u32[]{:S(2)}) async-start(f32[256,8,128]{2,1,0:T(8,128)} %bitcast.1), calls=%async_computation | async-start | bytes 2097152 | tf_op jit(solution)/shard_map/all_to_all | solution.py:282
  25.1 1.3 %copy-start.9 = (bf16[8,480,256]{2,1,0:T(8,128)(2,1)}, bf16[8,480,256]{2,1,0:T(8,128)(2,1)S(1)}, u32[]{:S(2)}) copy-start(bf16[8,480,256]{2,1,0:T(8,128)(2,1)S(1)} %get-tuple-element.7.w_ref) | copy-start | bytes 5898244
  53.3 1.5 %copy-start.10 = (bf16[8,480,256]{2,1,0:T(8,128)(2,1)S(1)}, bf16[8,480,256]{2,1,0:T(8,128)(2,1)}, u32[]{:S(2)}) copy-start(bf16[8,480,256]{2,1,0:T(8,128)(2,1)} %copy-done.9) | copy-start | bytes 5898244
  68.4 36.8 %copy-start = (f32[8,32,512]{2,1,0:T(8,128)S(1)}, f32[8,32,512]{2,1,0:T(8,128)}, u32[]{:S(2)}) copy-start(f32[8,32,512]{2,1,0:T(8,128)} %contrast_ref.1) | copy-start | bytes 1572868

commit v2 on v1

--- a/solution.py
+++ b/solution.py
@@ -1,4 +1,3 @@
-import functools
 import math
 
 import jax
@@ -19,6 +18,9 @@
 WINDOW = 40
 MIB = 1 << 20
 
+FACTOR_ROWS = 2 * PLANES + 3 * WINDOW
+ALL_FACTOR_ROWS = FACTOR_ROWS * LAYERS + PLANES
+
 
 def split_np(x):
     x = x.astype(np.float32)
@@ -32,7 +34,7 @@
     angle = 2.0 * math.pi / HALF * ((index[:, None] * index[None, :]) % HALF)
     hi, lo = split_np(np.concatenate([np.cos(angle), np.sin(angle)], 0))
     turn = 2.0 * math.pi / (2 * HALF) * index
-    return hi, lo, np.stack([np.cos(turn), np.sin(turn)]).astype(np.float32)
+    return np.concatenate([hi, lo], 0), np.stack([np.cos(turn), np.sin(turn)]).astype(np.float32)
 
 
 def split(x):
@@ -56,12 +58,22 @@
     return dot_nt(a_hi, b_hi) + dot_nt(a_hi, b_lo) + dot_nt(a_lo, b_hi)
 
 
-def forward_y_kernel(w_ref, hi_ref, lo_ref, tw_ref, o_ref):
+def forward_y_kernel(w_hbm, table_hbm, tw_hbm, o_ref, w_ref, table_ref, tw_ref, sems):
+    pairs = w_ref.shape[1] // 2
+    copies = [
+        pltpu.make_async_copy(w_hbm.at[:, pl.ds(2 * i, 2)], w_ref.at[:, pl.ds(2 * i, 2)], sems.at[i]) for i in range(pairs)
+    ]
+    fetch_tw = pltpu.make_async_copy(tw_hbm, tw_ref, sems.at[pairs])
+    fetch_table = pltpu.make_async_copy(table_hbm, table_ref, sems.at[pairs + 1])
+    for copy in (copies[0], fetch_tw, fetch_table, *copies[1:]):
+        copy.start()
+    fetch_tw.wait()
+    fetch_table.wait()
     cos, sin = tw_ref[0:1, :], tw_ref[1:2, :]
-    t_hi, t_lo = hi_ref[...], lo_ref[...]
+    t_hi, t_lo = table_ref[: 2 * HALF], table_ref[2 * HALF :]
     lane = lax.broadcasted_iota(jnp.int32, (HALF, 128), 1)
-    planes = w_ref.shape[1]
-    for pair in range(planes // 2):
+    for pair in range(pairs):
+        copies[pair].wait()
         rows = []
         for z in (2 * pair, 2 * pair + 1):
             first = [w_ref[c, z, :, :HALF] for c in (0, 1)]
@@ -120,6 +132,34 @@
         w_ref[l, 8 * WINDOW : 10 * WINDOW], w_ref[l, 10 * WINDOW :] = split(blocks(hre, him))
 
 
+def factors_kernel(rates_ref, start_ref, ky_ref, f_ref):
+    g = pl.program_id(0)
+
+    def signed(k):
+        return jnp.where(k >= HALF, k - 2 * HALF, k).astype(F32) / HALF
+
+    kx = 2 * lax.broadcasted_iota(jnp.int32, (1, HALF), 1) + g % 2
+    freq_y = signed(jnp.full((1, HALF), 2 * ky_ref[0] + g // 2, jnp.int32))
+    steep = jnp.sqrt(1.0 + signed(kx) ** 2 + freq_y**2)
+    plane = lax.broadcasted_iota(jnp.int32, (PLANES, HALF), 0).astype(F32)
+    window = lax.broadcasted_iota(jnp.int32, (WINDOW, HALF), 0).astype(F32)
+    own_depth = jnp.zeros((PLANES, HALF), F32)
+    for l in range(LAYERS):
+        depth = start_ref[l].astype(F32)
+        rate = rates_ref[l] / PLANES
+        own_depth = jnp.where(plane >= depth, (plane - depth) * rate, own_depth)
+        fall = rate * steep
+        at = FACTOR_ROWS * l
+        f_ref[0, at : at + PLANES] = jnp.exp(-jnp.abs(plane - depth) * fall)
+        f_ref[0, at + PLANES : at + 2 * PLANES] = jnp.exp(plane * (-0.5 * fall))
+        there = window + window_of(start_ref[l]).astype(F32)
+        at += 2 * PLANES
+        f_ref[0, at : at + WINDOW] = jnp.exp((depth - there) * fall)
+        f_ref[0, at + WINDOW : at + 2 * WINDOW] = jnp.exp((there - depth) * fall)
+        f_ref[0, at + 2 * WINDOW : at + 3 * WINDOW] = jnp.exp(there * (-0.5 * fall))
+    f_ref[0, FACTOR_ROWS * LAYERS :] = jnp.exp(own_depth * steep)
+
+
 def exchange(parts):
     piece = lax.broadcasted_iota(jnp.int32, parts[0].shape, 1) // 32
     turned = [x if i == 0 else pltpu.roll(x, 32 * i, 1) for i, x in enumerate(parts)]
@@ -133,9 +173,31 @@
 
 
 def middle_kernel(
-    rates_ref, start_ref, ky_ref, g_ref, hi_ref, lo_ref, tw_ref, w_ref, own_ref, o_ref, line, v_hi, v_lo, own, mixed, back
+    start_ref,
+    g_ref,
+    table_ref,
+    tw_ref,
+    w_hbm,
+    own_hbm,
+    f_hbm,
+    o_ref,
+    line,
+    spec,
+    own,
+    mixed,
+    back,
+    w_ref,
+    own_ref,
+    f_ref,
+    sems,
 ):
+    fetch_factors = [pltpu.make_async_copy(f_hbm.at[g], f_ref.at[g], sems.at[g]) for g in range(4)]
+    fetch_mix = pltpu.make_async_copy(w_hbm, w_ref, sems.at[4])
+    fetch_own = pltpu.make_async_copy(own_hbm, own_ref, sems.at[5])
+    for copy in (fetch_own, fetch_factors[0], fetch_mix, *fetch_factors[1:]):
+        copy.start()
     cos, sin = tw_ref[0:1, :], tw_ref[1:2, :]
+    t_hi, t_lo = table_ref[: 2 * HALF], table_ref[2 * HALF :]
     for group in range(4):
         parts = [g_ref[:, 4 * group + i].reshape(PLANES, 128) for i in range(4)]
         for q, x in enumerate(exchange(parts)):
@@ -143,72 +205,62 @@
     for ky in (0, 1):
         first = [line[c, ky, :, :HALF] for c in (0, 1)]
         second = [line[c, ky, :, HALF:] for c in (0, 1)]
+        even = [first[c] + second[c] for c in (0, 1)]
         odd = [first[c] - second[c] for c in (0, 1)]
         turned = (odd[0] * cos + odd[1] * sin, odd[1] * cos - odd[0] * sin)
-        for c in (0, 1):
-            rows = slice(PLANES * c, PLANES * (c + 1))
-            v_hi[2 * ky, rows], v_lo[2 * ky, rows] = split(first[c] + second[c])
-            v_hi[2 * ky + 1, rows], v_lo[2 * ky + 1, rows] = split(turned[c])
+        for parity, x in enumerate((even, turned)):
+            x_hi, x_lo = split(jnp.concatenate(x, 0))
+            out = dot3(x_hi, x_lo, t_hi, t_lo)
+            spec[2 * ky + parity, 0] = out[:PLANES, :HALF] + out[PLANES:, HALF:]
+            spec[2 * ky + parity, 1] = out[PLANES:, :HALF] - out[:PLANES, HALF:]
 
     own[:, PLANES:] = jnp.zeros((2, WINDOW, HALF), F32)
-    plane = lax.broadcasted_iota(jnp.int32, (PLANES, HALF), 0).astype(F32)
-    own_depth = jnp.zeros((PLANES, HALF), F32)
-    for l in range(LAYERS):
-        p = start_ref[l].astype(F32)
-        own_depth = jnp.where(plane >= p, (plane - p) * (rates_ref[l] / PLANES), own_depth)
-    window = lax.broadcasted_iota(jnp.int32, (WINDOW, HALF), 0).astype(F32)
-
-    def signed(k):
-        return jnp.where(k >= HALF, k - 2 * HALF, k).astype(F32) / HALF
+    plane = lax.broadcasted_iota(jnp.int32, (8, HALF), 0)
+    fetch_own.wait()
+    fetch_mix.wait()
 
     @pl.loop(0, 4)
     def _(g):
-        t_hi, t_lo = hi_ref[...], lo_ref[...]
-        out = dot3(v_hi[g], v_lo[g], t_hi, t_lo)
-        spec_re = out[:PLANES, :HALF] + out[PLANES:, HALF:]
-        spec_im = out[PLANES:, :HALF] - out[:PLANES, HALF:]
-        kx = 2 * lax.broadcasted_iota(jnp.int32, (1, HALF), 1) + g % 2
-        freq_y = signed(jnp.full((1, HALF), 2 * ky_ref[0] + g // 2, jnp.int32))
-        steep = jnp.sqrt(1.0 + signed(kx) ** 2 + freq_y**2)
-
-        def weighted(factor):
-            return split(jnp.concatenate([spec_re * factor, spec_im * factor], 0))
-
-        x_hi, x_lo = weighted(jnp.exp(own_depth * steep))
+        pltpu.make_async_copy(f_hbm.at[g], f_ref.at[g], sems.at[g]).wait()
+
+        def weighted(at):
+            factor = f_ref[g, at : at + PLANES]
+            return split(jnp.concatenate([spec[g, 0] * factor, spec[g, 1] * factor], 0))
+
+        x_hi, x_lo = weighted(FACTOR_ROWS * LAYERS)
         sums = dot_nn(own_ref[...], x_hi)
         sums = sums[: 2 * PLANES] + sums[2 * PLANES :] + dot_nn(own_ref[: 2 * PLANES], x_lo)
         own[0, :PLANES], own[1, :PLANES] = sums[:PLANES], sums[PLANES:]
         for l in range(LAYERS):
-            p = start_ref[l]
-            depth = p.astype(F32)
-            rate = rates_ref[l] / PLANES
-            x_hi, x_lo = weighted(jnp.exp((jnp.abs(plane - depth) * -rate) * steep))
+            at = FACTOR_ROWS * l
+            x_hi, x_lo = weighted(at)
             direct = dot_nn(w_ref[l, : 8 * WINDOW], x_hi)
             direct = direct[: 4 * WINDOW] + direct[4 * WINDOW :] + dot_nn(w_ref[l, : 4 * WINDOW], x_lo)
-            x_hi, x_lo = weighted(jnp.exp((plane * (-0.5 * rate)) * steep))
+            x_hi, x_lo = weighted(at + PLANES)
             reflected = dot_nn(w_ref[l, 8 * WINDOW :], x_hi)
             reflected = reflected[: 2 * WINDOW] + reflected[2 * WINDOW :] + dot_nn(w_ref[l, 8 * WINDOW : 10 * WINDOW], x_lo)
+            p = start_ref[l]
             q = window_of(p)
-            there = window + q.astype(F32)
-            angle = (there - depth) * (rate * steep)
-            fade, rise = jnp.exp(-angle), jnp.exp(angle)
-            far = jnp.exp(there * (-0.5 * rate * steep))
+            at += 2 * PLANES
+            fade, rise, far = (f_ref[g, at + WINDOW * i : at + WINDOW * (i + 1)] for i in range(3))
             for c in (0, 1):
                 rows = slice(WINDOW * c, WINDOW * (c + 1))
                 near = direct[rows] + own[c, pl.ds(q, WINDOW), :]
                 after = direct[2 * WINDOW + WINDOW * c : 3 * WINDOW + WINDOW * c]
                 sums = near * fade + after * rise + reflected[rows] * far
                 kept = mixed[c, pl.ds(q, 8), :]
-                mixed[c, pl.ds(q, 8), :] = jnp.where(there[:8] >= depth, sums[:8], kept)
+                mixed[c, pl.ds(q, 8), :] = jnp.where(plane + q >= p, sums[:8], kept)
                 mixed[c, pl.ds(pl.multiple_of(q + 8, 8), WINDOW - 8), :] = sums[8:]
-        m_hi, m_lo = split(jnp.concatenate([mixed[0, :PLANES], mixed[1, :PLANES]], 0))
-        inv = dot3(m_hi, m_lo, t_hi, t_lo)
-        back[g, 0] = inv[:PLANES, :HALF] - inv[PLANES:, HALF:]
-        back[g, 1] = inv[:PLANES, HALF:] + inv[PLANES:, :HALF]
+        for c in (0, 1):
+            back[g, c] = mixed[c, :PLANES]
 
     for ky in (0, 1):
-        even = [back[2 * ky, c] for c in (0, 1)]
-        odd = [back[2 * ky + 1, c] for c in (0, 1)]
+        halves = []
+        for parity in (0, 1):
+            m_hi, m_lo = split(jnp.concatenate([back[2 * ky + parity, 0], back[2 * ky + parity, 1]], 0))
+            inv = dot3(m_hi, m_lo, t_hi, t_lo)
+            halves.append((inv[:PLANES, :HALF] - inv[PLANES:, HALF:], inv[:PLANES, HALF:] + inv[PLANES:, :HALF]))
+        even, odd = halves
         turned = (odd[0] * cos - odd[1] * sin, odd[0] * sin + odd[1] * cos)
         for c in (0, 1):
             line[c, ky, :, :HALF] = even[c] + turned[c]
@@ -219,9 +271,10 @@
             o_ref[:, 4 * group + i] = x.reshape(PLANES // 8, 8, 128)
 
 
-def inverse_y_kernel(g_ref, contrast_ref, hi_ref, lo_ref, tw_ref, o_ref):
+def inverse_y_kernel(g_ref, contrast_ref, table_ref, tw_ref, o_hbm, o_ref, sems):
     cos, sin = tw_ref[0:1, :], tw_ref[1:2, :]
-    t_hi, t_lo = hi_ref[...], lo_ref[...]
+    t_hi, t_lo = table_ref[: 2 * HALF], table_ref[2 * HALF :]
+    copies = []
     planes = contrast_ref.shape[0]
     scale = 1.0 / (4 * HALF * HALF)
     for pair in range(planes // 2):
@@ -237,18 +290,26 @@
             for c, even in enumerate((re[:32], im[:32])):
                 o_ref[c, z, :, :HALF] = (even + turned[c]) * (contrast_ref[z, :, :HALF] * scale)
                 o_ref[c, z, :, HALF:] = (even - turned[c]) * (contrast_ref[z, :, HALF:] * scale)
-
-
-def vmem(count):
-    return [pl.BlockSpec(memory_space=pltpu.VMEM)] * count
-
-
-def call(kernel, out_shape, operands, flops, scalars=0, scratch=(), limit=16):
+        here = pl.ds(2 * pair, 2)
+        copies.append(pltpu.make_async_copy(o_ref.at[:, here], o_hbm.at[:, here], sems.at[pair]))
+        copies[-1].start()
+    for copy in copies:
+        copy.wait()
+
+
+VMEM = pl.BlockSpec(memory_space=pltpu.VMEM)
+SMEM = pl.BlockSpec(memory_space=pltpu.SMEM)
+HBM = pl.BlockSpec(memory_space=pltpu.HBM)
+
+
+def call(kernel, out_shape, operands, in_specs, out_specs, flops, scratch=(), limit=16, grid=()):
+    operands = [pltpu.with_memory_space_constraint(x, pltpu.HBM) if spec is HBM else x for x, spec in zip(operands, in_specs)]
     return pl.pallas_call(
         kernel,
+        grid=grid,
         out_shape=out_shape,
-        in_specs=[pl.BlockSpec(memory_space=pltpu.SMEM)] * scalars + vmem(len(operands) - scalars),
-        out_specs=jax.tree.map(lambda _: pl.BlockSpec(memory_space=pltpu.VMEM), out_shape),
+        in_specs=in_specs,
+        out_specs=out_specs,
         scratch_shapes=list(scratch),
         compiler_params=pltpu.CompilerParams(vmem_limit_bytes=limit * MIB),
         cost_estimate=pl.CostEstimate(flops=flops, bytes_accessed=4 * MIB, transcendentals=0),
@@ -256,52 +317,78 @@
 
 
 def body(wave_field, contrast, layer_of_plane, toeplitz_table, hankel_table, layer_rates):
-    t_hi, t_lo, turn = dft_tables()
-    t_hi, t_lo, turn = jnp.asarray(t_hi), jnp.asarray(t_lo), jnp.asarray(turn)
-    dft = (t_hi, t_lo, turn)
+    table, turn = (jnp.asarray(x) for x in dft_tables())
     ids = jnp.arange(LAYERS, dtype=jnp.int32)
     starts = jnp.sum((layer_of_plane[None, :] < ids[:, None]).astype(jnp.int32), axis=1)
     toeplitz = jnp.pad(toeplitz_table[:, :, ::-1], ((0, 0), (0, 0), (0, 1)))
     hankel = jnp.pad(hankel_table, ((0, 0), (0, 0), (0, 1)))
     ky_pair = (lax.axis_index("lay") * lax.axis_size("lat") + lax.axis_index("lat")).reshape(1)
-
-    tiles = jax.ShapeDtypeStruct((2 * HALF * 4, 128), F32)
-    sent = call(forward_y_kernel, tiles, (wave_field, *dft), 6 * 2**27)
+    planes = contrast.shape[0]
+    shape = jax.ShapeDtypeStruct
+    dma = pltpu.SemaphoreType.DMA
+
+    sent = call(
+        forward_y_kernel,
+        shape((2 * HALF * 4, 128), F32),
+        (wave_field, table, turn),
+        [HBM] * 3,
+        VMEM,
+        6 * 2**27,
+        scratch=(
+            pltpu.VMEM(wave_field.shape, F32),
+            pltpu.VMEM(table.shape, BF16),
+            pltpu.VMEM(turn.shape, F32),
+            dma((planes // 2 + 2,)),
+        ),
+    )
     window_mix, own_mix = call(
         tables_kernel,
-        (
-            jax.ShapeDtypeStruct((LAYERS, 12 * WINDOW, 2 * PLANES), BF16),
-            jax.ShapeDtypeStruct((4 * PLANES, 2 * PLANES), BF16),
-        ),
+        (shape((LAYERS, 12 * WINDOW, 2 * PLANES), BF16), shape((4 * PLANES, 2 * PLANES), BF16)),
         (starts, toeplitz, hankel),
-        2**28,
-        scalars=1,
+        [SMEM, VMEM, VMEM],
+        (VMEM, VMEM),
+        2**30,
         scratch=(pltpu.VMEM((4, PLANES + WINDOW, PLANES), F32),),
-        limit=12,
+    )
+    factors = call(
+        factors_kernel,
+        shape((4, ALL_FACTOR_ROWS, HALF), F32),
+        (layer_rates, starts, ky_pair),
+        [SMEM] * 3,
+        pl.BlockSpec((1, ALL_FACTOR_ROWS, HALF), lambda g: (g, 0, 0)),
+        2**32,
+        grid=(4,),
     )
     lines = lax.all_to_all(sent.reshape(HALF, 8, 128), AXES, 0, 0, tiled=True)
     lines = call(
         middle_kernel,
-        jax.ShapeDtypeStruct((16, 16, 8, 128), F32),
-        (layer_rates, starts, ky_pair, lines.reshape(16, 16, 8, 128), *dft, window_mix, own_mix),
+        shape((16, 16, 8, 128), F32),
+        (starts, lines.reshape(16, 16, 8, 128), table, turn, window_mix, own_mix, factors),
+        [SMEM, VMEM, VMEM, VMEM, HBM, HBM, HBM],
+        VMEM,
         2**32,
-        scalars=3,
         scratch=(
             pltpu.VMEM((2, 2, PLANES, 2 * HALF), F32),
-            pltpu.VMEM((4, 2 * PLANES, HALF), BF16),
-            pltpu.VMEM((4, 2 * PLANES, HALF), BF16),
+            pltpu.VMEM((4, 2, PLANES, HALF), F32),
             pltpu.VMEM((2, PLANES + WINDOW, HALF), F32),
             pltpu.VMEM((2, PLANES + WINDOW, HALF), F32),
             pltpu.VMEM((4, 2, PLANES, HALF), F32),
+            pltpu.VMEM(window_mix.shape, BF16),
+            pltpu.VMEM(own_mix.shape, BF16),
+            pltpu.VMEM(factors.shape, F32),
+            dma((6,)),
         ),
-        limit=20,
+        limit=32,
     )
     lines = lax.all_to_all(lines.reshape(HALF, 8, 128), AXES, 0, 0, tiled=True)
     return call(
         inverse_y_kernel,
-        jax.ShapeDtypeStruct(wave_field.shape, F32),
-        (lines.reshape(2 * HALF * 4, 128), contrast, *dft),
+        shape(wave_field.shape, F32),
+        (lines.reshape(2 * HALF * 4, 128), contrast, table, turn),
+        [VMEM] * 4,
+        HBM,
         6 * 2**27,
+        scratch=(pltpu.VMEM(wave_field.shape, F32), dma((planes // 2,))),
     )
 
 

time: 108 us -> 102 us (0.944)
  waiting for transfers between devices: 26.9 us -> 16.4 us
  Pallas kernels: 20.8 us -> 23.3 us
  local copies, waits for them, and re-layouts: 6.94 us -> 8.91 us
    all_to_all x1, waiting for transfers between devices: 26.9 us -> 16.4 us  [body(): lines = lax.all_to_all(sent.reshape(HALF, 8, 128), AXES, 0, 0, tiled=True)]
    pallas_call x4 -> x5, Pallas kernels: 20.8 us -> 23.3 us  [call(): pl.pallas_call(kernel, grid=grid, out_shape=out_shape, in_specs=in_specs,...]
    unnamed x30 -> x16, local copies, waits for them, and re-layouts: 6.92 us -> 8.17 us
  transfers between devices with their start and end apart: 1 -> 1, of which waited for: 1 -> 1; matrix products, arithmetic and copies ran while one was open for 0% -> 2% of each run, Pallas kernels for 3% -> 5%
where the time goes in v2:
time: 102 us
  blocking collectives  36.8 us (36%)
  Pallas kernels  23.3 us (23%)
  waiting for transfers between devices  16.4 us (16%)
  starting transfers between devices  15.7 us (15%)
  local copies, waits for them, and re-layouts  8.91 us (9%)
    all_to_all x1, blocking collectives, body(): lines = lax.all_to_all(lines.reshape(HALF, 8, 128), AXES, 0, 0, tiled=True)  36.8 us
    pallas_call x5, Pallas kernels, call(): pl.pallas_call(kernel, grid=grid, out_shape=out_shape, in_specs=in_specs,...  23.3 us
    all_to_all x1, waiting for transfers between devices, body(): lines = lax.all_to_all(sent.reshape(HALF, 8, 128), AXES, 0, 0, tiled=True)  16.4 us
    all_to_all x1, starting transfers between devices, body(): lines = lax.all_to_all(sent.reshape(HALF, 8, 128), AXES, 0, 0, tiled=True)  15.7 us
    unnamed x16, local copies, waits for them, and re-layouts  8.17 us
  transfers between devices with their start and end apart: 1, of which 1 were waited for; matrix products, arithmetic and copies ran while one was open for 2% of the time, Pallas kernels for 5%

profile of v2, /device:TPU:1, one launch (start us, length us, event | category | flops | bytes accessed | tf_op | source)
XLA Modules:
  0.0 101.9 jit_solution(3363761830872594073)
XLA Ops:
  0.0 0.0 copy-start.5
  0.0 0.0 copy-start.1
  0.0 4.9 %shard_map.82 = f32[2048,128]{1,0:T(8,128)} custom-call(f32[2,8,32,512]{3,2,1,0:T(8,128)} %w_hbm.1, bf16[1024,256]{1,0:T(8,128)(2,1)} %constant.17.clone.table_hbm.table_ref, f32[2,256]{1,0:T(2,128)} %constant.18.clone.tw_hbm.tw_ref), custom_call_target="tpu_custom_call" | custom-call | flops 805306368 | bytes 4194304 | tf_op jit(solution)/shard_map/pallas_call | solution.py:307
  4.9 15.7 %all-to-all-start = ((f32[256,8,128]{2,1,0:T(8,128)}), f32[256,8,128]{2,1,0:T(8,128)S(1)}, u32[]{:S(2)}, u32[]{:S(2)}) async-start(f32[256,8,128]{2,1,0:T(8,128)} %bitcast), calls=%async_computation | async-start | bytes 2097152 | tf_op jit(solution)/shard_map/all_to_all | solution.py:362
  20.6 0.8 reverse
  21.4 0.1 slice
  21.5 0.7 pad.8.han_ref
  22.3 0.8 convert_reduce_fusion.start_ref
  23.0 3.0 %shard_map.83 = (bf16[8,480,256]{2,1,0:T(8,128)(2,1)S(1)}, bf16[512,256]{1,0:T(8,128)(2,1)S(1)}) custom-call(s32[8]{0:T(128)S(1)} %convert_reduce_fusion.start_ref, f32[2,8,256]{2,1,0:T(8,128)S(1)} %pad.7.toe_ref, f32[2,8,256]{2,1,0:T(8,128)S(1)} %pad.8.han_ref), custom_call_target="tpu_custom_call" | custom-call | flops 1073741824 | bytes 4194304 | tf_op jit(solution)/shard_map/pallas_call | solution.py:307
  26.0 0.0 copy-start.2
  26.0 1.3 %copy-done.2 = bf16[8,480,256]{2,1,0:T(8,128)(2,1)} copy-done((bf16[8,480,256]{2,1,0:T(8,128)(2,1)}, bf16[8,480,256]{2,1,0:T(8,128)(2,1)S(1)}, u32[]{:S(2)}) %copy-start.2) | copy-done | bytes 1966104
  27.3 0.0 copy-start.4
  27.3 0.7 copy-done.4
  28.0 0.0 copy-start.6
  28.0 0.7 copy-done.6
  28.7 2.6 %shard_map.84.f_hbm = f32[4,3136,256]{2,1,0:T(8,128)S(1)} custom-call(f32[8]{0:T(128)S(1)} %copy-done.6, s32[8]{0:T(128)S(1)} %convert_reduce_fusion.start_ref, s32[1]{0:T(128)} %bitcast.2.ky_ref), custom_call_target="tpu_custom_call" | custom-call | flops 4294967296 | bytes 4194304 | tf_op jit(solution)/shard_map/pallas_call | solution.py:307
  31.3 0.0 copy-start
  31.3 4.6 %copy-done = f32[4,3136,256]{2,1,0:T(8,128)} copy-done((f32[4,3136,256]{2,1,0:T(8,128)}, f32[4,3136,256]{2,1,0:T(8,128)S(1)}, u32[]{:S(2)}) %copy-start) | copy-done | bytes 12845080
  35.9 0.0 copy-start.3
  35.9 16.4 %all-to-all-done = f32[256,8,128]{2,1,0:T(8,128)S(1)} async-done(((f32[256,8,128]{2,1,0:T(8,128)}), f32[256,8,128]{2,1,0:T(8,128)S(1)}, u32[]{:S(2)}, u32[]{:S(2)}) %all-to-all-start) | async-done | bytes 1048608 | tf_op jit(solution)/shard_map/all_to_all | solution.py:362
  52.3 0.0 copy-done.5
  52.3 0.0 copy-done.1
  52.3 10.9 %shard_map.85 = f32[16,16,8,128]{3,2,1,0:T(8,128)S(1)} custom-call(s32[8]{0:T(128)S(1)} %convert_reduce_fusion.start_ref, f32[16,16,8,128]{3,2,1,0:T(8,128)S(1)} %bitcast.7, bf16[1024,256]{1,0:T(8,128)(2,1)S(1)} %copy-done.1, f32[2,256]{1,0:T(2,128)S(1)} %copy-done.5, bf16[8,480,256]{2,1,0:T(8,128)(2,1)} %copy-done.2, bf16[512,256]{1,0:T(8,128)(2,1)} %copy-done.4, ...), custom_call_target="tpu_custom_call" | custom-call | flops 4294967296 | bytes 4194304 | tf_op jit(solution)/shard_map/pallas_call | solution.py:307
  63.1 36.8 %all_to_all.10 = f32[256,8,128]{2,1,0:T(8,128)S(1)} all-to-all(f32[256,8,128]{2,1,0:T(8,128)S(1)} %bitcast.8), channel_id=1, replica_groups=mesh['lat'=16,'lay'=16] {'lay','lat'}, dimensions={0} | all-to-all | bytes 2097152 | tf_op jit(solution)/shard_map/all_to_all | solution.py:383
  99.9 0.0 copy-done.3
  99.9 1.9 %shard_map.86 = f32[2,8,32,512]{3,2,1,0:T(8,128)} custom-call(f32[2048,128]{1,0:T(8,128)S(1)} %bitcast.6, f32[8,32,512]{2,1,0:T(8,128)S(1)} %copy-done.3, bf16[1024,256]{1,0:T(8,128)(2,1)S(1)} %copy-done.1, f32[2,256]{1,0:T(2,128)S(1)} %copy-done.5), custom_call_target="tpu_custom_call" | custom-call | flops 805306368 | bytes 4194304 | tf_op jit(solution)/shard_map/pallas_call | solution.py:307
  (1 shorter events, 0.0 us)
Async XLA Ops:
  0.0 52.3 %copy-start.5 = (f32[2,256]{1,0:T(2,128)S(1)}, f32[2,256]{1,0:T(2,128)}, u32[]{:S(2)}) copy-start(f32[2,256]{1,0:T(2,128)} %constant.18.clone.tw_hbm.tw_ref) | copy-start | bytes 6148
  0.0 52.3 %copy-start.1 = (bf16[1024,256]{1,0:T(8,128)(2,1)S(1)}, bf16[1024,256]{1,0:T(8,128)(2,1)}, u32[]{:S(2)}) copy-start(bf16[1024,256]{1,0:T(8,128)(2,1)} %constant.17.clone.table_hbm.table_ref) | copy-start | bytes 1572868
  4.9 47.3 %all-to-all-start = ((f32[256,8,128]{2,1,0:T(8,128)}), f32[256,8,128]{2,1,0:T(8,128)S(1)}, u32[]{:S(2)}, u32[]{:S(2)}) async-start(f32[256,8,128]{2,1,0:T(8,128)} %bitcast), calls=%async_computation | async-start | bytes 2097152 | tf_op jit(solution)/shard_map/all_to_all | solution.py:362
  26.0 1.3 %copy-start.2 = (bf16[8,480,256]{2,1,0:T(8,128)(2,1)}, bf16[8,480,256]{2,1,0:T(8,128)(2,1)S(1)}, u32[]{:S(2)}) copy-start(bf16[8,480,256]{2,1,0:T(8,128)(2,1)S(1)} %get-tuple-element.7.w_hbm) | copy-start | bytes 5898244
  27.3 0.7 copy-start.4
  28.0 0.7 copy-start.6
  31.3 4.6 %copy-start = (f32[4,3136,256]{2,1,0:T(8,128)}, f32[4,3136,256]{2,1,0:T(8,128)S(1)}, u32[]{:S(2)}) copy-start(f32[4,3136,256]{2,1,0:T(8,128)S(1)} %shard_map.84.f_hbm) | copy-start | bytes 38535172
  35.9 64.0 %copy-start.3 = (f32[8,32,512]{2,1,0:T(8,128)S(1)}, f32[8,32,512]{2,1,0:T(8,128)}, u32[]{:S(2)}) copy-start(f32[8,32,512]{2,1,0:T(8,128)} %contrast_ref.1) | copy-start | bytes 1572868

commit v3 on v2

--- a/solution.py
+++ b/solution.py
@@ -20,6 +20,9 @@
 
 FACTOR_ROWS = 2 * PLANES + 3 * WINDOW
 ALL_FACTOR_ROWS = FACTOR_ROWS * LAYERS + PLANES
+MIX_ROWS = 12 * WINDOW
+OWN_AT = MIX_ROWS * LAYERS
+SENDS = 2
 
 
 def split_np(x):
@@ -58,20 +61,17 @@
     return dot_nt(a_hi, b_hi) + dot_nt(a_hi, b_lo) + dot_nt(a_lo, b_hi)
 
 
-def forward_y_kernel(w_hbm, table_hbm, tw_hbm, o_ref, w_ref, table_ref, tw_ref, sems):
+def forward_y_kernel(w_hbm, table_hbm, tw_hbm, o_hbm, w_ref, table_ref, tw_ref, v_hi, v_lo, o_ref, sems):
     pairs = w_ref.shape[1] // 2
     copies = [
         pltpu.make_async_copy(w_hbm.at[:, pl.ds(2 * i, 2)], w_ref.at[:, pl.ds(2 * i, 2)], sems.at[i]) for i in range(pairs)
     ]
     fetch_tw = pltpu.make_async_copy(tw_hbm, tw_ref, sems.at[pairs])
     fetch_table = pltpu.make_async_copy(table_hbm, table_ref, sems.at[pairs + 1])
-    for copy in (copies[0], fetch_tw, fetch_table, *copies[1:]):
+    for copy in (fetch_tw, copies[0], fetch_table, *copies[1:]):
         copy.start()
     fetch_tw.wait()
-    fetch_table.wait()
     cos, sin = tw_ref[0:1, :], tw_ref[1:2, :]
-    t_hi, t_lo = table_ref[: 2 * HALF], table_ref[2 * HALF :]
-    lane = lax.broadcasted_iota(jnp.int32, (HALF, 128), 1)
     for pair in range(pairs):
         copies[pair].wait()
         rows = []
@@ -83,15 +83,32 @@
             odd_re = odd[0] * cos + odd[1] * sin
             odd_im = odd[1] * cos - odd[0] * sin
             rows += [even[0], odd_re, even[1], odd_im]
-        v_hi, v_lo = split(jnp.concatenate(rows, 0))
-        out = dot3(t_hi, t_lo, v_hi, v_lo)
-        for k in (0, 1):
-            with_cos = out[:HALF, 128 * k : 128 * (k + 1)]
-            with_sin = pltpu.roll(out[HALF:, 128 * k : 128 * (k + 1)], 64, 1)
-            o_ref[pl.ds(2 * pair + k, HALF, stride=8), :] = with_cos + jnp.where(lane < 64, with_sin, -with_sin)
-
-
-def tables_kernel(start_ref, toe_ref, han_ref, w_ref, own_ref, plane_rows):
+        v_hi[pair], v_lo[pair] = split(jnp.concatenate(rows, 0))
+    fetch_table.wait()
+    count = HALF // SENDS
+    lane = lax.broadcasted_iota(jnp.int32, (count, 128), 1)
+    sends = []
+    for part in range(SENDS):
+        cos_rows, sin_rows = slice(count * part, count * (part + 1)), slice(HALF + count * part, HALF + count * (part + 1))
+        t_hi = jnp.concatenate([table_ref[cos_rows], table_ref[sin_rows]], 0)
+        low = 2 * HALF
+        t_lo = jnp.concatenate([table_ref[low + rows.start : low + rows.stop] for rows in (cos_rows, sin_rows)], 0)
+        for pair in range(pairs):
+            out = dot3(t_hi, t_lo, v_hi[pair], v_lo[pair])
+            for k in (0, 1):
+                with_cos = out[:count, 128 * k : 128 * (k + 1)]
+                with_sin = pltpu.roll(out[count:, 128 * k : 128 * (k + 1)], 64, 1)
+                o_ref[pl.ds(8 * count * part + 2 * pair + k, count, stride=8), :] = with_cos + jnp.where(
+                    lane < 64, with_sin, -with_sin
+                )
+        here = pl.ds(8 * count * part, 8 * count)
+        sends.append(pltpu.make_async_copy(o_ref.at[here], o_hbm.at[here], sems.at[pairs + 2 + part]))
+        sends[-1].start()
+    for send in sends:
+        send.wait()
+
+
+def tables_kernel(start_ref, toe_ref, han_ref, mix_ref, same_start_ref, plane_rows):
     row = lax.broadcasted_iota(jnp.int32, (PLANES, 2 * PLANES), 0)
 
     def spread(ref, c, amount):
@@ -117,7 +134,7 @@
         first = jnp.where(z >= start_ref[l], start_ref[l], first)
     inside = (s >= first) & (s <= z)
     hi, lo = split(blocks(*(jnp.where(inside, plane_rows[c, :PLANES], 0.0) for c in (0, 1))))
-    own_ref[: 2 * PLANES], own_ref[2 * PLANES :] = hi, lo
+    mix_ref[OWN_AT : OWN_AT + 2 * PLANES], mix_ref[OWN_AT + 2 * PLANES :] = hi, lo
     j = lax.broadcasted_iota(jnp.int32, (WINDOW, PLANES), 0)
     s = lax.broadcasted_iota(jnp.int32, (WINDOW, PLANES), 1)
     for l in range(LAYERS):
@@ -128,8 +145,10 @@
         before = blocks(jnp.where(s < p, re, 0.0), jnp.where(s < p, im, 0.0))
         after = blocks(jnp.where(s > later, re, 0.0), jnp.where(s > later, im, 0.0))
         hi, lo = split(jnp.concatenate([before, after], 0))
-        w_ref[l, : 4 * WINDOW], w_ref[l, 4 * WINDOW : 8 * WINDOW] = hi, lo
-        w_ref[l, 8 * WINDOW : 10 * WINDOW], w_ref[l, 10 * WINDOW :] = split(blocks(hre, him))
+        at = MIX_ROWS * l
+        mix_ref[at : at + 4 * WINDOW], mix_ref[at + 4 * WINDOW : at + 8 * WINDOW] = hi, lo
+        mix_ref[at + 8 * WINDOW : at + 10 * WINDOW], mix_ref[at + 10 * WINDOW : at + 12 * WINDOW] = split(blocks(hre, him))
+        same_start_ref[l] = p
 
 
 def factors_kernel(rates_ref, start_ref, ky_ref, f_ref):
@@ -175,33 +194,30 @@
 def middle_kernel(
     start_ref,
     g_ref,
-    table_ref,
+    table_hbm,
     tw_ref,
-    w_hbm,
-    own_hbm,
+    mix_ref,
     f_hbm,
     o_ref,
     line,
     spec,
     own,
     mixed,
-    back,
-    w_ref,
-    own_ref,
     f_ref,
+    table_ref,
     sems,
 ):
-    fetch_factors = [pltpu.make_async_copy(f_hbm.at[g], f_ref.at[g], sems.at[g]) for g in range(4)]
-    fetch_mix = pltpu.make_async_copy(w_hbm, w_ref, sems.at[4])
-    fetch_own = pltpu.make_async_copy(own_hbm, own_ref, sems.at[5])
-    for copy in (fetch_own, fetch_factors[0], fetch_mix, *fetch_factors[1:]):
-        copy.start()
+    fetch_table = pltpu.make_async_copy(table_hbm, table_ref, sems.at[4])
+    fetch_table.start()
+    for g in range(4):
+        pltpu.make_async_copy(f_hbm.at[g], f_ref.at[g], sems.at[g]).start()
     cos, sin = tw_ref[0:1, :], tw_ref[1:2, :]
-    t_hi, t_lo = table_ref[: 2 * HALF], table_ref[2 * HALF :]
     for group in range(4):
         parts = [g_ref[:, 4 * group + i].reshape(PLANES, 128) for i in range(4)]
         for q, x in enumerate(exchange(parts)):
             line[q // 2, q % 2, :, 128 * group : 128 * (group + 1)] = x
+    fetch_table.wait()
+    t_hi, t_lo = table_ref[: 2 * HALF], table_ref[2 * HALF :]
     for ky in (0, 1):
         first = [line[c, ky, :, :HALF] for c in (0, 1)]
         second = [line[c, ky, :, HALF:] for c in (0, 1)]
@@ -214,10 +230,8 @@
             spec[2 * ky + parity, 0] = out[:PLANES, :HALF] + out[PLANES:, HALF:]
             spec[2 * ky + parity, 1] = out[PLANES:, :HALF] - out[:PLANES, HALF:]
 
-    own[:, PLANES:] = jnp.zeros((2, WINDOW, HALF), F32)
+    own[:, :, PLANES:] = jnp.zeros((4, 2, WINDOW, HALF), F32)
     plane = lax.broadcasted_iota(jnp.int32, (8, HALF), 0)
-    fetch_own.wait()
-    fetch_mix.wait()
 
     @pl.loop(0, 4)
     def _(g):
@@ -228,36 +242,34 @@
             return split(jnp.concatenate([spec[g, 0] * factor, spec[g, 1] * factor], 0))
 
         x_hi, x_lo = weighted(FACTOR_ROWS * LAYERS)
-        sums = dot_nn(own_ref[...], x_hi)
-        sums = sums[: 2 * PLANES] + sums[2 * PLANES :] + dot_nn(own_ref[: 2 * PLANES], x_lo)
-        own[0, :PLANES], own[1, :PLANES] = sums[:PLANES], sums[PLANES:]
+        sums = dot_nn(mix_ref[OWN_AT:], x_hi)
+        sums = sums[: 2 * PLANES] + sums[2 * PLANES :] + dot_nn(mix_ref[OWN_AT : OWN_AT + 2 * PLANES], x_lo)
+        own[g, 0, :PLANES], own[g, 1, :PLANES] = sums[:PLANES], sums[PLANES:]
         for l in range(LAYERS):
-            at = FACTOR_ROWS * l
+            at, row = FACTOR_ROWS * l, MIX_ROWS * l
             x_hi, x_lo = weighted(at)
-            direct = dot_nn(w_ref[l, : 8 * WINDOW], x_hi)
-            direct = direct[: 4 * WINDOW] + direct[4 * WINDOW :] + dot_nn(w_ref[l, : 4 * WINDOW], x_lo)
+            direct = dot_nn(mix_ref[row : row + 8 * WINDOW], x_hi)
+            direct = direct[: 4 * WINDOW] + direct[4 * WINDOW :] + dot_nn(mix_ref[row : row + 4 * WINDOW], x_lo)
             x_hi, x_lo = weighted(at + PLANES)
-            reflected = dot_nn(w_ref[l, 8 * WINDOW :], x_hi)
-            reflected = reflected[: 2 * WINDOW] + reflected[2 * WINDOW :] + dot_nn(w_ref[l, 8 * WINDOW : 10 * WINDOW], x_lo)
+            reflected = dot_nn(mix_ref[row + 8 * WINDOW : row + 12 * WINDOW], x_hi)
+            reflected = reflected[: 2 * WINDOW] + reflected[2 * WINDOW :] + dot_nn(mix_ref[row + 8 * WINDOW : row + 10 * WINDOW], x_lo)
             p = start_ref[l]
             q = window_of(p)
             at += 2 * PLANES
             fade, rise, far = (f_ref[g, at + WINDOW * i : at + WINDOW * (i + 1)] for i in range(3))
             for c in (0, 1):
                 rows = slice(WINDOW * c, WINDOW * (c + 1))
-                near = direct[rows] + own[c, pl.ds(q, WINDOW), :]
+                near = direct[rows] + own[g, c, pl.ds(q, WINDOW), :]
                 after = direct[2 * WINDOW + WINDOW * c : 3 * WINDOW + WINDOW * c]
                 sums = near * fade + after * rise + reflected[rows] * far
-                kept = mixed[c, pl.ds(q, 8), :]
-                mixed[c, pl.ds(q, 8), :] = jnp.where(plane + q >= p, sums[:8], kept)
-                mixed[c, pl.ds(pl.multiple_of(q + 8, 8), WINDOW - 8), :] = sums[8:]
-        for c in (0, 1):
-            back[g, c] = mixed[c, :PLANES]
+                kept = mixed[g, c, pl.ds(q, 8), :]
+                mixed[g, c, pl.ds(q, 8), :] = jnp.where(plane + q >= p, sums[:8], kept)
+                mixed[g, c, pl.ds(pl.multiple_of(q + 8, 8), WINDOW - 8), :] = sums[8:]
 
     for ky in (0, 1):
         halves = []
         for parity in (0, 1):
-            m_hi, m_lo = split(jnp.concatenate([back[2 * ky + parity, 0], back[2 * ky + parity, 1]], 0))
+            m_hi, m_lo = split(jnp.concatenate([mixed[2 * ky + parity, c, :PLANES] for c in (0, 1)], 0))
             inv = dot3(m_hi, m_lo, t_hi, t_lo)
             halves.append((inv[:PLANES, :HALF] - inv[PLANES:, HALF:], inv[:PLANES, HALF:] + inv[PLANES:, :HALF]))
         even, odd = halves
@@ -332,28 +344,32 @@
         shape((2 * HALF * 4, 128), F32),
         (wave_field, table, turn),
         [HBM] * 3,
-        VMEM,
+        HBM,
         6 * 2**27,
         scratch=(
             pltpu.VMEM(wave_field.shape, F32),
             pltpu.VMEM(table.shape, BF16),
             pltpu.VMEM(turn.shape, F32),
-            dma((planes // 2 + 2,)),
+            pltpu.VMEM((planes // 2, HALF, HALF), BF16),
+            pltpu.VMEM((planes // 2, HALF, HALF), BF16),
+            pltpu.VMEM((2 * HALF * 4, 128), F32),
+            dma((planes // 2 + 2 + SENDS,)),
         ),
     )
-    window_mix, own_mix = call(
+    mix, same_starts = call(
         tables_kernel,
-        (shape((LAYERS, 12 * WINDOW, 2 * PLANES), BF16), shape((4 * PLANES, 2 * PLANES), BF16)),
+        (pltpu.HBM((OWN_AT + 4 * PLANES, 2 * PLANES), BF16), shape((LAYERS,), jnp.int32)),
         (starts, toeplitz, hankel),
         [SMEM, VMEM, VMEM],
-        (VMEM, VMEM),
+        (pl.BlockSpec((OWN_AT + 4 * PLANES, 2 * PLANES), lambda i: (0, 0)), SMEM),
         2**30,
+        grid=(1,),
         scratch=(pltpu.VMEM((4, PLANES + WINDOW, PLANES), F32),),
     )
     factors = call(
         factors_kernel,
-        shape((4, ALL_FACTOR_ROWS, HALF), F32),
-        (layer_rates, starts, ky_pair),
+        pltpu.HBM((4, ALL_FACTOR_ROWS, HALF), F32),
+        (layer_rates, same_starts, ky_pair),
         [SMEM] * 3,
         pl.BlockSpec((1, ALL_FACTOR_ROWS, HALF), lambda g: (g, 0, 0)),
         2**32,
@@ -363,22 +379,20 @@
     lines = call(
         middle_kernel,
         shape((16, 16, 8, 128), F32),
-        (starts, lines.reshape(16, 16, 8, 128), table, turn, window_mix, own_mix, factors),
-        [SMEM, VMEM, VMEM, VMEM, HBM, HBM, HBM],
+        (starts, lines.reshape(16, 16, 8, 128), table, turn, mix, factors),
+        [SMEM, VMEM, HBM, VMEM, VMEM, HBM],
         VMEM,
         2**32,
         scratch=(
             pltpu.VMEM((2, 2, PLANES, 2 * HALF), F32),
             pltpu.VMEM((4, 2, PLANES, HALF), F32),
-            pltpu.VMEM((2, PLANES + WINDOW, HALF), F32),
-            pltpu.VMEM((2, PLANES + WINDOW, HALF), F32),
-            pltpu.VMEM((4, 2, PLANES, HALF), F32),
-            pltpu.VMEM(window_mix.shape, BF16),
-            pltpu.VMEM(own_mix.shape, BF16),
+            pltpu.VMEM((4, 2, PLANES + WINDOW, HALF), F32),
+            pltpu.VMEM((4, 2, PLANES + WINDOW, HALF), F32),
             pltpu.VMEM(factors.shape, F32),
-            dma((6,)),
+            pltpu.VMEM(table.shape, BF16),
+            dma((5,)),
         ),
-        limit=32,
+        limit=24,
     )
     lines = lax.all_to_all(lines.reshape(HALF, 8, 128), AXES, 0, 0, tiled=True)
     return call(

time: 102 us -> 99.7 us (0.977)
  local copies, waits for them, and re-layouts: 8.91 us -> 2.47 us
  Pallas kernels: 23.3 us -> 25.4 us
  waiting for transfers between devices: 16.4 us -> 18.1 us
    unnamed x16 -> x12, local copies, waits for them, and re-layouts: 8.17 us -> 1.73 us
    pallas_call x5, Pallas kernels: 23.3 us -> 25.4 us  [call(): pl.pallas_call(kernel, grid=grid, out_shape=out_shape, in_specs=in_specs,...]
    all_to_all x1, waiting for transfers between devices: 16.4 us -> 18.1 us  [body(): lines = lax.all_to_all(sent.reshape(HALF, 8, 128), AXES, 0, 0, tiled=True)]
  transfers between devices with their start and end apart: 1 -> 1, of which waited for: 1 -> 1; matrix products, arithmetic and copies ran while one was open for 2% -> 2% of each run, Pallas kernels for 5% -> 10%
where the time goes in v3:
time: 99.7 us; the launch traced here: 99.3 us
  blocking collectives  36.8 us (37%)
  Pallas kernels  25.4 us (25%)
  waiting for transfers between devices  18.1 us (18%)
  starting transfers between devices  15.7 us (16%)
  local copies, waits for them, and re-layouts  2.47 us (2%)
    all_to_all x1, blocking collectives, body(): lines = lax.all_to_all(lines.reshape(HALF, 8, 128), AXES, 0, 0, tiled=True)  36.8 us
    pallas_call x5, Pallas kernels, call(): pl.pallas_call(kernel, grid=grid, out_shape=out_shape, in_specs=in_specs,...  25.4 us
    all_to_all x1, waiting for transfers between devices, body(): lines = lax.all_to_all(sent.reshape(HALF, 8, 128), AXES, 0, 0, tiled=True)  18.1 us
    all_to_all x1, starting transfers between devices, body(): lines = lax.all_to_all(sent.reshape(HALF, 8, 128), AXES, 0, 0, tiled=True)  15.7 us
  transfers between devices with their start and end apart: 1, of which 1 were waited for; matrix products, arithmetic and copies ran while one was open for 2% of the time, Pallas kernels for 10%

profile of v3, /device:TPU:1, one launch (start us, length us, event | category | flops | bytes accessed | tf_op | source)
XLA Modules:
  0.0 99.3 jit_solution(8362730304315964353)
XLA Ops:
  0.0 0.0 copy-start.3
  0.0 3.4 %shard_map.82 = f32[2048,128]{1,0:T(8,128)} custom-call(f32[2,8,32,512]{3,2,1,0:T(8,128)} %w_hbm.1, bf16[1024,256]{1,0:T(8,128)(2,1)} %constant.17.clone.table_hbm.table_ref, f32[2,256]{1,0:T(2,128)} %constant.18.clone.tw_hbm.tw_ref), custom_call_target="tpu_custom_call" | custom-call | flops 805306368 | bytes 4194304 | tf_op jit(solution)/shard_map/pallas_call | solution.py:319
  3.4 15.7 %all-to-all-start = ((f32[256,8,128]{2,1,0:T(8,128)}), f32[256,8,128]{2,1,0:T(8,128)S(1)}, u32[]{:S(2)}, u32[]{:S(2)}) async-start(f32[256,8,128]{2,1,0:T(8,128)} %bitcast), calls=%async_computation | async-start | bytes 2097152 | tf_op jit(solution)/shard_map/all_to_all | solution.py:378
  19.1 0.8 reverse
  19.9 0.1 slice
  20.0 0.7 pad.8.han_ref
  20.8 0.8 convert_reduce_fusion.start_ref
  21.5 4.4 %shard_map.83 = (bf16[4352,256]{1,0:T(8,128)(2,1)}, s32[8]{0:T(128)S(1)}) custom-call(s32[8]{0:T(128)S(1)} %convert_reduce_fusion.start_ref, f32[2,8,256]{2,1,0:T(8,128)S(1)} %pad.7.toe_ref, f32[2,8,256]{2,1,0:T(8,128)S(1)} %pad.8.han_ref), custom_call_target="tpu_custom_call" | custom-call | flops 1073741824 | bytes 4194304 | tf_op jit(solution)/shard_map/pallas_call | solution.py:319
  25.9 0.0 copy-start
  25.9 0.0 copy-start.4
  25.9 0.8 copy-done.4
  26.7 5.9 %shard_map.84.f_hbm = f32[4,3136,256]{2,1,0:T(8,128)} custom-call(f32[8]{0:T(128)S(1)} %copy-done.4, s32[8]{0:T(128)S(1)} %get-tuple-element.8.start_ref, s32[1]{0:T(128)} %bitcast.2.ky_ref), custom_call_target="tpu_custom_call" | custom-call | flops 4294967296 | bytes 4194304 | tf_op jit(solution)/shard_map/pallas_call | solution.py:319
  32.6 18.1 %all-to-all-done = f32[256,8,128]{2,1,0:T(8,128)S(1)} async-done(((f32[256,8,128]{2,1,0:T(8,128)}), f32[256,8,128]{2,1,0:T(8,128)S(1)}, u32[]{:S(2)}, u32[]{:S(2)}) %all-to-all-start) | async-done | bytes 1048608 | tf_op jit(solution)/shard_map/all_to_all | solution.py:378
  50.7 0.0 copy-start.1
  50.7 0.0 copy-start.2
  50.7 0.0 copy-done.3
  50.7 0.0 copy-done
  50.8 9.8 %shard_map.85 = f32[16,16,8,128]{3,2,1,0:T(8,128)S(1)} custom-call(s32[8]{0:T(128)S(1)} %convert_reduce_fusion.start_ref, f32[16,16,8,128]{3,2,1,0:T(8,128)S(1)} %bitcast.7, bf16[1024,256]{1,0:T(8,128)(2,1)} %constant.17.clone.table_hbm.table_ref, f32[2,256]{1,0:T(2,128)S(1)} %copy-done.3, bf16[4352,256]{1,0:T(8,128)(2,1)S(1)} %copy-done, ...), custom_call_target="tpu_custom_call" | custom-call | flops 4294967296 | bytes 4194304 | tf_op jit(solution)/shard_map/pallas_call | solution.py:319
  60.6 36.8 %all_to_all.10 = f32[256,8,128]{2,1,0:T(8,128)S(1)} all-to-all(f32[256,8,128]{2,1,0:T(8,128)S(1)} %bitcast.8), channel_id=1, replica_groups=mesh['lat'=16,'lay'=16] {'lay','lat'}, dimensions={0} | all-to-all | bytes 2097152 | tf_op jit(solution)/shard_map/all_to_all | solution.py:397
  97.3 0.0 copy-done.1
  97.4 0.0 copy-done.2
  97.4 2.0 %shard_map.86 = f32[2,8,32,512]{3,2,1,0:T(8,128)} custom-call(f32[2048,128]{1,0:T(8,128)S(1)} %bitcast.6, f32[8,32,512]{2,1,0:T(8,128)S(1)} %copy-done.2, bf16[1024,256]{1,0:T(8,128)(2,1)S(1)} %copy-done.1, f32[2,256]{1,0:T(2,128)S(1)} %copy-done.3), custom_call_target="tpu_custom_call" | custom-call | flops 805306368 | bytes 4194304 | tf_op jit(solution)/shard_map/pallas_call | solution.py:319
  (1 shorter events, 0.0 us)
Async XLA Ops:
  0.0 50.7 %copy-start.3 = (f32[2,256]{1,0:T(2,128)S(1)}, f32[2,256]{1,0:T(2,128)}, u32[]{:S(2)}) copy-start(f32[2,256]{1,0:T(2,128)} %constant.18.clone.tw_hbm.tw_ref) | copy-start | bytes 6148
  3.4 47.3 %all-to-all-start = ((f32[256,8,128]{2,1,0:T(8,128)}), f32[256,8,128]{2,1,0:T(8,128)S(1)}, u32[]{:S(2)}, u32[]{:S(2)}) async-start(f32[256,8,128]{2,1,0:T(8,128)} %bitcast), calls=%async_computation | async-start | bytes 2097152 | tf_op jit(solution)/shard_map/all_to_all | solution.py:378
  25.9 24.8 %copy-start = (bf16[4352,256]{1,0:T(8,128)(2,1)S(1)}, bf16[4352,256]{1,0:T(8,128)(2,1)}, u32[]{:S(2)}) copy-start(bf16[4352,256]{1,0:T(8,128)(2,1)} %get-tuple-element.7.mix_ref) | copy-start | bytes 6684676
  25.9 0.8 copy-start.4
  50.7 46.6 %copy-start.1 = (bf16[1024,256]{1,0:T(8,128)(2,1)S(1)}, bf16[1024,256]{1,0:T(8,128)(2,1)}, u32[]{:S(2)}) copy-start(bf16[1024,256]{1,0:T(8,128)(2,1)} %constant.17.clone.table_hbm.table_ref) | copy-start | bytes 1572868
  50.7 46.6 %copy-start.2 = (f32[8,32,512]{2,1,0:T(8,128)S(1)}, f32[8,32,512]{2,1,0:T(8,128)}, u32[]{:S(2)}) copy-start(f32[8,32,512]{2,1,0:T(8,128)} %contrast_ref.1) | copy-start | bytes 1572868

commit v4 on v3

--- a/solution.py
+++ b/solution.py
@@ -13,6 +13,7 @@
 F32 = jnp.float32
 BF16 = jnp.bfloat16
 HALF = 256
+QUARTER = 128
 PLANES = 128
 LAYERS = 8
 WINDOW = 40
@@ -22,7 +23,7 @@
 ALL_FACTOR_ROWS = FACTOR_ROWS * LAYERS + PLANES
 MIX_ROWS = 12 * WINDOW
 OWN_AT = MIX_ROWS * LAYERS
-SENDS = 2
+SENDS = 1
 
 
 def split_np(x):
@@ -33,11 +34,12 @@
 
 
 def dft_tables():
-    index = np.arange(HALF)
-    angle = 2.0 * math.pi / HALF * ((index[:, None] * index[None, :]) % HALF)
-    hi, lo = split_np(np.concatenate([np.cos(angle), np.sin(angle)], 0))
-    turn = 2.0 * math.pi / (2 * HALF) * index
-    return np.concatenate([hi, lo], 0), np.stack([np.cos(turn), np.sin(turn)]).astype(np.float32)
+    index = np.arange(QUARTER)
+    angle = 2.0 * math.pi / QUARTER * ((index[:, None] * index[None, :]) % QUARTER)
+    cos, sin = np.cos(angle), np.sin(angle)
+    hi, lo = split_np(np.block([[cos, sin], [-sin, cos]]))
+    turn = 2.0 * math.pi / (4 * QUARTER) * np.arange(4)[:, None] * index[None, :]
+    return np.concatenate([hi, lo], 0), np.concatenate([np.cos(turn), np.sin(turn)], 0).astype(np.float32)
 
 
 def split(x):
@@ -57,8 +59,46 @@
     return jnp.dot(a, b, preferred_element_type=F32)
 
 
-def dot3(a_hi, a_lo, b_hi, b_lo):
-    return dot_nt(a_hi, b_hi) + dot_nt(a_hi, b_lo) + dot_nt(a_lo, b_hi)
+def dot3(dot, a, b):
+    return dot(a[0], b[0]) + dot(a[0], b[1]) + dot(a[1], b[0])
+
+
+def radix_forward(quarters, tw_ref):
+    (a_re, a_im), (b_re, b_im), (c_re, c_im), (d_re, d_im) = quarters
+    ac_re, ac_im, bd_re, bd_im = a_re + c_re, a_im + c_im, b_re + d_re, b_im + d_im
+    am_re, am_im, bm_re, bm_im = a_re - c_re, a_im - c_im, b_re - d_re, b_im - d_im
+    out = [
+        (ac_re + bd_re, ac_im + bd_im),
+        (am_re + bm_im, am_im - bm_re),
+        (ac_re - bd_re, ac_im - bd_im),
+        (am_re - bm_im, am_im + bm_re),
+    ]
+    for r in range(1, 4):
+        cos, sin = tw_ref[r : r + 1, :], tw_ref[4 + r : 5 + r, :]
+        re, im = out[r]
+        out[r] = (re * cos + im * sin, im * cos - re * sin)
+    return out
+
+
+def radix_inverse(residues, tw_ref):
+    turned = [residues[0]]
+    for r in range(1, 4):
+        cos, sin = tw_ref[r : r + 1, :], tw_ref[4 + r : 5 + r, :]
+        re, im = residues[r]
+        turned.append((re * cos - im * sin, re * sin + im * cos))
+    (a_re, a_im), (b_re, b_im), (c_re, c_im), (d_re, d_im) = turned
+    ac_re, ac_im, bd_re, bd_im = a_re + c_re, a_im + c_im, b_re + d_re, b_im + d_im
+    am_re, am_im, bm_re, bm_im = a_re - c_re, a_im - c_im, b_re - d_re, b_im - d_im
+    return [
+        (ac_re + bd_re, ac_im + bd_im),
+        (am_re - bm_im, am_im + bm_re),
+        (ac_re - bd_re, ac_im - bd_im),
+        (am_re + bm_im, am_im - bm_re),
+    ]
+
+
+def quarter(h):
+    return slice(QUARTER * h, QUARTER * (h + 1))
 
 
 def forward_y_kernel(w_hbm, table_hbm, tw_hbm, o_hbm, w_ref, table_ref, tw_ref, v_hi, v_lo, o_ref, sems):
@@ -71,37 +111,32 @@
     for copy in (fetch_tw, copies[0], fetch_table, *copies[1:]):
         copy.start()
     fetch_tw.wait()
-    cos, sin = tw_ref[0:1, :], tw_ref[1:2, :]
     for pair in range(pairs):
         copies[pair].wait()
         rows = []
         for z in (2 * pair, 2 * pair + 1):
-            first = [w_ref[c, z, :, :HALF] for c in (0, 1)]
-            second = [w_ref[c, z, :, HALF:] for c in (0, 1)]
-            even = [first[c] + second[c] for c in (0, 1)]
-            odd = [first[c] - second[c] for c in (0, 1)]
-            odd_re = odd[0] * cos + odd[1] * sin
-            odd_im = odd[1] * cos - odd[0] * sin
-            rows += [even[0], odd_re, even[1], odd_im]
+            quarters = [[w_ref[c, z, :, quarter(h)] for c in (0, 1)] for h in range(4)]
+            rows += [jnp.concatenate(x, 1) for x in radix_forward(quarters, tw_ref)]
         v_hi[pair], v_lo[pair] = split(jnp.concatenate(rows, 0))
     fetch_table.wait()
-    count = HALF // SENDS
+    count = QUARTER // SENDS
     lane = lax.broadcasted_iota(jnp.int32, (count, 128), 1)
     sends = []
     for part in range(SENDS):
-        cos_rows, sin_rows = slice(count * part, count * (part + 1)), slice(HALF + count * part, HALF + count * (part + 1))
-        t_hi = jnp.concatenate([table_ref[cos_rows], table_ref[sin_rows]], 0)
-        low = 2 * HALF
-        t_lo = jnp.concatenate([table_ref[low + rows.start : low + rows.stop] for rows in (cos_rows, sin_rows)], 0)
+        at = count * part
+        table = [
+            jnp.concatenate([table_ref[low + at : low + at + count], table_ref[low + QUARTER + at : low + QUARTER + at + count]], 0)
+            for low in (0, HALF)
+        ]
         for pair in range(pairs):
-            out = dot3(t_hi, t_lo, v_hi[pair], v_lo[pair])
+            out = dot3(dot_nt, table, (v_hi[pair], v_lo[pair]))
             for k in (0, 1):
-                with_cos = out[:count, 128 * k : 128 * (k + 1)]
-                with_sin = pltpu.roll(out[count:, 128 * k : 128 * (k + 1)], 64, 1)
-                o_ref[pl.ds(8 * count * part + 2 * pair + k, count, stride=8), :] = with_cos + jnp.where(
-                    lane < 64, with_sin, -with_sin
-                )
-        here = pl.ds(8 * count * part, 8 * count)
+                re, im = out[:count, 128 * k : 128 * (k + 1)], out[count:, 128 * k : 128 * (k + 1)]
+                swapped = pltpu.roll(jnp.where(lane < 64, im, re), 64, 1)
+                first = 16 * at + 2 * pair + k
+                o_ref[pl.ds(first, count, stride=16), :] = jnp.where(lane < 64, re, swapped)
+                o_ref[pl.ds(first + 8, count, stride=16), :] = jnp.where(lane < 64, swapped, im)
+        here = pl.ds(16 * at, 16 * count)
         sends.append(pltpu.make_async_copy(o_ref.at[here], o_hbm.at[here], sems.at[pairs + 2 + part]))
         sends[-1].start()
     for send in sends:
@@ -157,7 +192,8 @@
     def signed(k):
         return jnp.where(k >= HALF, k - 2 * HALF, k).astype(F32) / HALF
 
-    kx = 2 * lax.broadcasted_iota(jnp.int32, (1, HALF), 1) + g % 2
+    lane = lax.broadcasted_iota(jnp.int32, (1, HALF), 1)
+    kx = 4 * (lane & (QUARTER - 1)) + 2 * (g % 2) + (lane >> 7)
     freq_y = signed(jnp.full((1, HALF), 2 * ky_ref[0] + g // 2, jnp.int32))
     steep = jnp.sqrt(1.0 + signed(kx) ** 2 + freq_y**2)
     plane = lax.broadcasted_iota(jnp.int32, (PLANES, HALF), 0).astype(F32)
@@ -211,24 +247,19 @@
     fetch_table.start()
     for g in range(4):
         pltpu.make_async_copy(f_hbm.at[g], f_ref.at[g], sems.at[g]).start()
-    cos, sin = tw_ref[0:1, :], tw_ref[1:2, :]
     for group in range(4):
         parts = [g_ref[:, 4 * group + i].reshape(PLANES, 128) for i in range(4)]
         for q, x in enumerate(exchange(parts)):
             line[q // 2, q % 2, :, 128 * group : 128 * (group + 1)] = x
     fetch_table.wait()
-    t_hi, t_lo = table_ref[: 2 * HALF], table_ref[2 * HALF :]
+    table = (table_ref[:HALF], table_ref[HALF:])
     for ky in (0, 1):
-        first = [line[c, ky, :, :HALF] for c in (0, 1)]
-        second = [line[c, ky, :, HALF:] for c in (0, 1)]
-        even = [first[c] + second[c] for c in (0, 1)]
-        odd = [first[c] - second[c] for c in (0, 1)]
-        turned = (odd[0] * cos + odd[1] * sin, odd[1] * cos - odd[0] * sin)
-        for parity, x in enumerate((even, turned)):
-            x_hi, x_lo = split(jnp.concatenate(x, 0))
-            out = dot3(x_hi, x_lo, t_hi, t_lo)
-            spec[2 * ky + parity, 0] = out[:PLANES, :HALF] + out[PLANES:, HALF:]
-            spec[2 * ky + parity, 1] = out[PLANES:, :HALF] - out[:PLANES, HALF:]
+        quarters = [[line[c, ky, :, quarter(h)] for c in (0, 1)] for h in range(4)]
+        x = jnp.concatenate([jnp.concatenate(v, 1) for v in radix_forward(quarters, tw_ref)], 0)
+        out = dot3(dot_nt, split(x), table)
+        for r in range(4):
+            for c in (0, 1):
+                spec[2 * ky + r // 2, c, :, quarter(r % 2)] = out[quarter(r), quarter(c)]
 
     own[:, :, PLANES:] = jnp.zeros((4, 2, WINDOW, HALF), F32)
     plane = lax.broadcasted_iota(jnp.int32, (8, HALF), 0)
@@ -267,16 +298,18 @@
                 mixed[g, c, pl.ds(pl.multiple_of(q + 8, 8), WINDOW - 8), :] = sums[8:]
 
     for ky in (0, 1):
-        halves = []
-        for parity in (0, 1):
-            m_hi, m_lo = split(jnp.concatenate([mixed[2 * ky + parity, c, :PLANES] for c in (0, 1)], 0))
-            inv = dot3(m_hi, m_lo, t_hi, t_lo)
-            halves.append((inv[:PLANES, :HALF] - inv[PLANES:, HALF:], inv[:PLANES, HALF:] + inv[PLANES:, :HALF]))
-        even, odd = halves
-        turned = (odd[0] * cos - odd[1] * sin, odd[0] * sin + odd[1] * cos)
-        for c in (0, 1):
-            line[c, ky, :, :HALF] = even[c] + turned[c]
-            line[c, ky, :, HALF:] = even[c] - turned[c]
+        x = jnp.concatenate(
+            [
+                jnp.concatenate([mixed[2 * ky + r // 2, c, :PLANES, quarter(r % 2)] for c in (0, 1)], 1)
+                for r in range(4)
+            ],
+            0,
+        )
+        out = dot3(dot_nn, split(x), table)
+        residues = [[out[quarter(r), quarter(c)] for c in (0, 1)] for r in range(4)]
+        for h, x in enumerate(radix_inverse(residues, tw_ref)):
+            for c in (0, 1):
+                line[c, ky, :, quarter(h)] = x[c]
     for group in range(4):
         parts = [line[q // 2, q % 2, :, 128 * group : 128 * (group + 1)] for q in range(4)]
         for i, x in enumerate(exchange(parts)):
@@ -284,24 +317,25 @@
 
 
 def inverse_y_kernel(g_ref, contrast_ref, table_ref, tw_ref, o_hbm, o_ref, sems):
-    cos, sin = tw_ref[0:1, :], tw_ref[1:2, :]
-    t_hi, t_lo = table_ref[: 2 * HALF], table_ref[2 * HALF :]
+    table = (table_ref[:HALF], table_ref[HALF:])
     copies = []
     planes = contrast_ref.shape[0]
     scale = 1.0 / (4 * HALF * HALF)
     for pair in range(planes // 2):
-        both = [jnp.transpose(g_ref[pl.ds(2 * pair + k, HALF, stride=8), :]) for k in (0, 1)]
-        m_hi, m_lo = split(jnp.concatenate(both, 0))
-        out = dot3(m_hi, m_lo, t_hi, t_lo)
+        rows = []
+        for z in (2 * pair, 2 * pair + 1):
+            for high in (0, 1):
+                x = jnp.transpose(g_ref[pl.ds(8 * high + z, QUARTER, stride=16), :])
+                rows.append(jnp.concatenate([x[:64], x[64:]], 1))
+        out = dot3(dot_nn, split(jnp.concatenate(rows, 0)), table)
         for k in (0, 1):
-            real, imag = out[128 * k : 128 * k + 64], out[128 * k + 64 : 128 * (k + 1)]
-            re = real[:, :HALF] - imag[:, HALF:]
-            im = real[:, HALF:] + imag[:, :HALF]
-            turned = (re[32:] * cos - im[32:] * sin, re[32:] * sin + im[32:] * cos)
             z = 2 * pair + k
-            for c, even in enumerate((re[:32], im[:32])):
-                o_ref[c, z, :, :HALF] = (even + turned[c]) * (contrast_ref[z, :, :HALF] * scale)
-                o_ref[c, z, :, HALF:] = (even - turned[c]) * (contrast_ref[z, :, HALF:] * scale)
+            at = 128 * k
+            residues = [[out[at + 32 * r : at + 32 * (r + 1), quarter(c)] for c in (0, 1)] for r in range(4)]
+            for h, x in enumerate(radix_inverse(residues, tw_ref)):
+                weight = contrast_ref[z, :, quarter(h)] * scale
+                for c in (0, 1):
+                    o_ref[c, z, :, quarter(h)] = x[c] * weight
         here = pl.ds(2 * pair, 2)
         copies.append(pltpu.make_async_copy(o_ref.at[:, here], o_hbm.at[:, here], sems.at[pair]))
         copies[-1].start()

time: 99.7 us -> 98.8 us (level)
  no operation moved by 1% of the time
where the time goes in v4:
time: 98.8 us; the launch traced here: 98.4 us
  blocking collectives  36.8 us (37%)
  Pallas kernels  24.6 us (25%)
  waiting for transfers between devices  18.1 us (18%)
  starting transfers between devices  15.7 us (16%)
  local copies, waits for them, and re-layouts  2.47 us (3%)
    all_to_all x1, blocking collectives, body(): lines = lax.all_to_all(lines.reshape(HALF, 8, 128), AXES, 0, 0, tiled=True)  36.8 us
    pallas_call x5, Pallas kernels, call(): pl.pallas_call(kernel, grid=grid, out_shape=out_shape, in_specs=in_specs,...  24.6 us
    all_to_all x1, waiting for transfers between devices, body(): lines = lax.all_to_all(sent.reshape(HALF, 8, 128), AXES, 0, 0, tiled=True)  18.1 us
    all_to_all x1, starting transfers between devices, body(): lines = lax.all_to_all(sent.reshape(HALF, 8, 128), AXES, 0, 0, tiled=True)  15.7 us
  transfers between devices with their start and end apart: 1, of which 1 were waited for; matrix products, arithmetic and copies ran while one was open for 2% of the time, Pallas kernels for 10%

profile of v4, /device:TPU:1, one launch (start us, length us, event | category | flops | bytes accessed | tf_op | source)
XLA Modules:
  0.0 98.4 jit_solution(1011988339627668412)
XLA Ops:
  0.0 0.0 copy-start.2
  0.0 3.2 %shard_map.82 = f32[2048,128]{1,0:T(8,128)} custom-call(f32[2,8,32,512]{3,2,1,0:T(8,128)} %w_hbm.1, bf16[512,256]{1,0:T(8,128)(2,1)} %constant.17.clone.table_hbm.table_ref, f32[8,128]{1,0:T(8,128)} %constant.18.clone.tw_hbm.tw_ref), custom_call_target="tpu_custom_call" | custom-call | flops 805306368 | bytes 4194304 | tf_op jit(solution)/shard_map/pallas_call | solution.py:353
  3.3 15.7 %all-to-all-start = ((f32[256,8,128]{2,1,0:T(8,128)}), f32[256,8,128]{2,1,0:T(8,128)S(1)}, u32[]{:S(2)}, u32[]{:S(2)}) async-start(f32[256,8,128]{2,1,0:T(8,128)} %bitcast), calls=%async_computation | async-start | bytes 2097152 | tf_op jit(solution)/shard_map/all_to_all | solution.py:412
  18.9 0.8 reverse
  19.8 0.1 slice
  19.9 0.7 pad.8.han_ref
  20.6 0.8 convert_reduce_fusion.start_ref
  21.4 4.4 %shard_map.83 = (bf16[4352,256]{1,0:T(8,128)(2,1)}, s32[8]{0:T(128)S(1)}) custom-call(s32[8]{0:T(128)S(1)} %convert_reduce_fusion.start_ref, f32[2,8,256]{2,1,0:T(8,128)S(1)} %pad.7.toe_ref, f32[2,8,256]{2,1,0:T(8,128)S(1)} %pad.8.han_ref), custom_call_target="tpu_custom_call" | custom-call | flops 1073741824 | bytes 4194304 | tf_op jit(solution)/shard_map/pallas_call | solution.py:353
  25.7 0.0 copy-start
  25.8 0.0 copy-start.4
  25.8 0.8 copy-done.4
  26.6 5.9 %shard_map.84.f_hbm = f32[4,3136,256]{2,1,0:T(8,128)} custom-call(f32[8]{0:T(128)S(1)} %copy-done.4, s32[8]{0:T(128)S(1)} %get-tuple-element.8.start_ref, s32[1]{0:T(128)} %bitcast.2.ky_ref), custom_call_target="tpu_custom_call" | custom-call | flops 4294967296 | bytes 4194304 | tf_op jit(solution)/shard_map/pallas_call | solution.py:353
  32.5 0.0 copy-start.1
  32.5 18.1 %all-to-all-done = f32[256,8,128]{2,1,0:T(8,128)S(1)} async-done(((f32[256,8,128]{2,1,0:T(8,128)}), f32[256,8,128]{2,1,0:T(8,128)S(1)}, u32[]{:S(2)}, u32[]{:S(2)}) %all-to-all-start) | async-done | bytes 1048608 | tf_op jit(solution)/shard_map/all_to_all | solution.py:412
  50.6 0.0 copy-start.3
  50.6 0.0 copy-done.2
  50.6 0.0 copy-done
  50.6 9.4 %shard_map.85 = f32[16,16,8,128]{3,2,1,0:T(8,128)S(1)} custom-call(s32[8]{0:T(128)S(1)} %convert_reduce_fusion.start_ref, f32[16,16,8,128]{3,2,1,0:T(8,128)S(1)} %bitcast.6, bf16[512,256]{1,0:T(8,128)(2,1)} %constant.17.clone.table_hbm.table_ref, f32[8,128]{1,0:T(8,128)S(1)} %copy-done.2, bf16[4352,256]{1,0:T(8,128)(2,1)S(1)} %copy-done, ...), custom_call_target="tpu_custom_call" | custom-call | flops 4294967296 | bytes 4194304 | tf_op jit(solution)/shard_map/pallas_call | solution.py:353
  60.0 36.8 %all_to_all.10 = f32[256,8,128]{2,1,0:T(8,128)S(1)} all-to-all(f32[256,8,128]{2,1,0:T(8,128)S(1)} %bitcast.7), channel_id=1, replica_groups=mesh['lat'=16,'lay'=16] {'lay','lat'}, dimensions={0} | all-to-all | bytes 2097152 | tf_op jit(solution)/shard_map/all_to_all | solution.py:431
  96.7 0.0 copy-done.1
  96.7 0.0 copy-done.3
  96.7 1.7 %shard_map.86 = f32[2,8,32,512]{3,2,1,0:T(8,128)} custom-call(f32[2048,128]{1,0:T(8,128)S(1)} %bitcast.8, f32[8,32,512]{2,1,0:T(8,128)S(1)} %copy-done.3, bf16[512,256]{1,0:T(8,128)(2,1)S(1)} %copy-done.1, f32[8,128]{1,0:T(8,128)S(1)} %copy-done.2), custom_call_target="tpu_custom_call" | custom-call | flops 805306368 | bytes 4194304 | tf_op jit(solution)/shard_map/pallas_call | solution.py:353
  (1 shorter events, 0.0 us)
Async XLA Ops:
  0.0 50.6 %copy-start.2 = (f32[8,128]{1,0:T(8,128)S(1)}, f32[8,128]{1,0:T(8,128)}, u32[]{:S(2)}) copy-start(f32[8,128]{1,0:T(8,128)} %constant.18.clone.tw_hbm.tw_ref) | copy-start | bytes 12292
  3.3 47.3 %all-to-all-start = ((f32[256,8,128]{2,1,0:T(8,128)}), f32[256,8,128]{2,1,0:T(8,128)S(1)}, u32[]{:S(2)}, u32[]{:S(2)}) async-start(f32[256,8,128]{2,1,0:T(8,128)} %bitcast), calls=%async_computation | async-start | bytes 2097152 | tf_op jit(solution)/shard_map/all_to_all | solution.py:412
  25.7 24.8 %copy-start = (bf16[4352,256]{1,0:T(8,128)(2,1)S(1)}, bf16[4352,256]{1,0:T(8,128)(2,1)}, u32[]{:S(2)}) copy-start(bf16[4352,256]{1,0:T(8,128)(2,1)} %get-tuple-element.7.mix_ref) | copy-start | bytes 6684676
  25.8 0.8 copy-start.4
  32.5 64.3 %copy-start.1 = (bf16[512,256]{1,0:T(8,128)(2,1)S(1)}, bf16[512,256]{1,0:T(8,128)(2,1)}, u32[]{:S(2)}) copy-start(bf16[512,256]{1,0:T(8,128)(2,1)} %constant.17.clone.table_hbm.table_ref) | copy-start | bytes 786436
  50.6 46.2 %copy-start.3 = (f32[8,32,512]{2,1,0:T(8,128)S(1)}, f32[8,32,512]{2,1,0:T(8,128)}, u32[]{:S(2)}) copy-start(f32[8,32,512]{2,1,0:T(8,128)} %contrast_ref.1) | copy-start | bytes 1572868

commit v5 on v4

--- a/solution.py
+++ b/solution.py
@@ -20,7 +20,7 @@
 MIB = 1 << 20
 
 FACTOR_ROWS = 2 * PLANES + 3 * WINDOW
-ALL_FACTOR_ROWS = FACTOR_ROWS * LAYERS + PLANES
+ALL_FACTOR_ROWS = FACTOR_ROWS * LAYERS
 MIX_ROWS = 12 * WINDOW
 OWN_AT = MIX_ROWS * LAYERS
 SENDS = 1
@@ -186,7 +186,7 @@
         same_start_ref[l] = p
 
 
-def factors_kernel(rates_ref, start_ref, ky_ref, f_ref):
+def factors_kernel(rates_ref, start_ref, ky_ref, f_ref, own_f_ref):
     g = pl.program_id(0)
 
     def signed(k):
@@ -212,7 +212,7 @@
         f_ref[0, at : at + WINDOW] = jnp.exp((depth - there) * fall)
         f_ref[0, at + WINDOW : at + 2 * WINDOW] = jnp.exp((there - depth) * fall)
         f_ref[0, at + 2 * WINDOW : at + 3 * WINDOW] = jnp.exp(there * (-0.5 * fall))
-    f_ref[0, FACTOR_ROWS * LAYERS :] = jnp.exp(own_depth * steep)
+    own_f_ref[0] = jnp.exp(own_depth * steep)
 
 
 def exchange(parts):
@@ -234,17 +234,21 @@
     tw_ref,
     mix_ref,
     f_hbm,
+    own_f_hbm,
     o_ref,
     line,
     spec,
     own,
     mixed,
     f_ref,
+    own_f_ref,
     table_ref,
     sems,
 ):
     fetch_table = pltpu.make_async_copy(table_hbm, table_ref, sems.at[4])
     fetch_table.start()
+    fetch_own = pltpu.make_async_copy(own_f_hbm, own_f_ref, sems.at[5])
+    fetch_own.start()
     for g in range(4):
         pltpu.make_async_copy(f_hbm.at[g], f_ref.at[g], sems.at[g]).start()
     for group in range(4):
@@ -263,6 +267,12 @@
 
     own[:, :, PLANES:] = jnp.zeros((4, 2, WINDOW, HALF), F32)
     plane = lax.broadcasted_iota(jnp.int32, (8, HALF), 0)
+    fetch_own.wait()
+    for g in range(4):
+        x_hi, x_lo = split(jnp.concatenate([spec[g, 0] * own_f_ref[g], spec[g, 1] * own_f_ref[g]], 0))
+        sums = dot_nn(mix_ref[OWN_AT:], x_hi)
+        sums = sums[: 2 * PLANES] + sums[2 * PLANES :] + dot_nn(mix_ref[OWN_AT : OWN_AT + 2 * PLANES], x_lo)
+        own[g, 0, :PLANES], own[g, 1, :PLANES] = sums[:PLANES], sums[PLANES:]
 
     @pl.loop(0, 4)
     def _(g):
@@ -272,10 +282,6 @@
             factor = f_ref[g, at : at + PLANES]
             return split(jnp.concatenate([spec[g, 0] * factor, spec[g, 1] * factor], 0))
 
-        x_hi, x_lo = weighted(FACTOR_ROWS * LAYERS)
-        sums = dot_nn(mix_ref[OWN_AT:], x_hi)
-        sums = sums[: 2 * PLANES] + sums[2 * PLANES :] + dot_nn(mix_ref[OWN_AT : OWN_AT + 2 * PLANES], x_lo)
-        own[g, 0, :PLANES], own[g, 1, :PLANES] = sums[:PLANES], sums[PLANES:]
         for l in range(LAYERS):
             at, row = FACTOR_ROWS * l, MIX_ROWS * l
             x_hi, x_lo = weighted(at)
@@ -400,12 +406,15 @@
         grid=(1,),
         scratch=(pltpu.VMEM((4, PLANES + WINDOW, PLANES), F32),),
     )
-    factors = call(
+    factors, own_factors = call(
         factors_kernel,
-        pltpu.HBM((4, ALL_FACTOR_ROWS, HALF), F32),
+        (pltpu.HBM((4, ALL_FACTOR_ROWS, HALF), F32), pltpu.HBM((4, PLANES, HALF), F32)),
         (layer_rates, same_starts, ky_pair),
         [SMEM] * 3,
-        pl.BlockSpec((1, ALL_FACTOR_ROWS, HALF), lambda g: (g, 0, 0)),
+        (
+            pl.BlockSpec((1, ALL_FACTOR_ROWS, HALF), lambda g: (g, 0, 0)),
+            pl.BlockSpec((1, PLANES, HALF), lambda g: (g, 0, 0)),
+        ),
         2**32,
         grid=(4,),
     )
@@ -413,8 +422,8 @@
     lines = call(
         middle_kernel,
         shape((16, 16, 8, 128), F32),
-        (starts, lines.reshape(16, 16, 8, 128), table, turn, mix, factors),
-        [SMEM, VMEM, HBM, VMEM, VMEM, HBM],
+        (starts, lines.reshape(16, 16, 8, 128), table, turn, mix, factors, own_factors),
+        [SMEM, VMEM, HBM, VMEM, VMEM, HBM, HBM],
         VMEM,
         2**32,
         scratch=(
@@ -423,8 +432,9 @@
             pltpu.VMEM((4, 2, PLANES + WINDOW, HALF), F32),
             pltpu.VMEM((4, 2, PLANES + WINDOW, HALF), F32),
             pltpu.VMEM(factors.shape, F32),
+            pltpu.VMEM(own_factors.shape, F32),
             pltpu.VMEM(table.shape, BF16),
-            dma((5,)),
+            dma((6,)),
         ),
         limit=24,
     )

time: 98.8 us -> 98.7 us (level)
  no operation moved by 1% of the time
where the time goes in v5:
time: 98.7 us; the launch traced here: 98.4 us
  blocking collectives  36.8 us (37%)
  Pallas kernels  24.5 us (25%)
  waiting for transfers between devices  18.1 us (18%)
  starting transfers between devices  15.7 us (16%)
  local copies, waits for them, and re-layouts  2.47 us (3%)
    all_to_all x1, blocking collectives, body(): lines = lax.all_to_all(lines.reshape(HALF, 8, 128), AXES, 0, 0, tiled=True)  36.8 us
    pallas_call x5, Pallas kernels, call(): pl.pallas_call(kernel, grid=grid, out_shape=out_shape, in_specs=in_specs,...  24.5 us
    all_to_all x1, waiting for transfers between devices, body(): lines = lax.all_to_all(sent.reshape(HALF, 8, 128), AXES, 0, 0, tiled=True)  18.1 us
    all_to_all x1, starting transfers between devices, body(): lines = lax.all_to_all(sent.reshape(HALF, 8, 128), AXES, 0, 0, tiled=True)  15.7 us
  transfers between devices with their start and end apart: 1, of which 1 were waited for; matrix products, arithmetic and copies ran while one was open for 2% of the time, Pallas kernels for 10%

profile of v5, /device:TPU:1, one launch (start us, length us, event | category | flops | bytes accessed | tf_op | source)
XLA Modules:
  0.0 98.4 jit_solution(12261312208482491213)
XLA Ops:
  0.0 0.0 copy-start.2
  0.0 3.2 %shard_map.82 = f32[2048,128]{1,0:T(8,128)} custom-call(f32[2,8,32,512]{3,2,1,0:T(8,128)} %w_hbm.1, bf16[512,256]{1,0:T(8,128)(2,1)} %constant.17.clone.table_hbm.table_ref, f32[8,128]{1,0:T(8,128)} %constant.18.clone.tw_hbm.tw_ref), custom_call_target="tpu_custom_call" | custom-call | flops 805306368 | bytes 4194304 | tf_op jit(solution)/shard_map/pallas_call | solution.py:359
  3.3 15.7 %all-to-all-start = ((f32[256,8,128]{2,1,0:T(8,128)}), f32[256,8,128]{2,1,0:T(8,128)S(1)}, u32[]{:S(2)}, u32[]{:S(2)}) async-start(f32[256,8,128]{2,1,0:T(8,128)} %bitcast), calls=%async_computation | async-start | bytes 2097152 | tf_op jit(solution)/shard_map/all_to_all | solution.py:421
  18.9 0.8 reverse
  19.8 0.1 slice
  19.9 0.7 pad.8.han_ref
  20.6 0.8 convert_reduce_fusion.start_ref
  21.4 4.5 %shard_map.83 = (bf16[4352,256]{1,0:T(8,128)(2,1)}, s32[8]{0:T(128)S(1)}) custom-call(s32[8]{0:T(128)S(1)} %convert_reduce_fusion.start_ref, f32[2,8,256]{2,1,0:T(8,128)S(1)} %pad.7.toe_ref, f32[2,8,256]{2,1,0:T(8,128)S(1)} %pad.8.han_ref), custom_call_target="tpu_custom_call" | custom-call | flops 1073741824 | bytes 4194304 | tf_op jit(solution)/shard_map/pallas_call | solution.py:359
  25.8 0.0 copy-start
  25.8 0.0 copy-start.4
  25.8 0.8 copy-done.4
  26.6 5.8 %shard_map.84 = (f32[4,3008,256]{2,1,0:T(8,128)}, f32[4,128,256]{2,1,0:T(8,128)}) custom-call(f32[8]{0:T(128)S(1)} %copy-done.4, s32[8]{0:T(128)S(1)} %get-tuple-element.10.start_ref, s32[1]{0:T(128)} %bitcast.2.ky_ref), custom_call_target="tpu_custom_call" | custom-call | flops 4294967296 | bytes 4194304 | tf_op jit(solution)/shard_map/pallas_call | solution.py:359
  32.5 0.0 copy-start.1
  32.5 18.1 %all-to-all-done = f32[256,8,128]{2,1,0:T(8,128)S(1)} async-done(((f32[256,8,128]{2,1,0:T(8,128)}), f32[256,8,128]{2,1,0:T(8,128)S(1)}, u32[]{:S(2)}, u32[]{:S(2)}) %all-to-all-start) | async-done | bytes 1048608 | tf_op jit(solution)/shard_map/all_to_all | solution.py:421
  50.6 0.0 copy-start.3
  50.6 0.0 copy-done.2
  50.6 0.0 copy-done
  50.6 9.3 %shard_map.85 = f32[16,16,8,128]{3,2,1,0:T(8,128)S(1)} custom-call(s32[8]{0:T(128)S(1)} %convert_reduce_fusion.start_ref, f32[16,16,8,128]{3,2,1,0:T(8,128)S(1)} %bitcast.6, bf16[512,256]{1,0:T(8,128)(2,1)} %constant.17.clone.table_hbm.table_ref, f32[8,128]{1,0:T(8,128)S(1)} %copy-done.2, bf16[4352,256]{1,0:T(8,128)(2,1)S(1)} %copy-done, ...), custom_call_target="tpu_custom_call" | custom-call | flops 4294967296 | bytes 4194304 | tf_op jit(solution)/shard_map/pallas_call | solution.py:359
  59.9 36.8 %all_to_all.10 = f32[256,8,128]{2,1,0:T(8,128)S(1)} all-to-all(f32[256,8,128]{2,1,0:T(8,128)S(1)} %bitcast.7), channel_id=1, replica_groups=mesh['lat'=16,'lay'=16] {'lay','lat'}, dimensions={0} | all-to-all | bytes 2097152 | tf_op jit(solution)/shard_map/all_to_all | solution.py:441
  96.7 0.0 copy-done.1
  96.7 0.0 copy-done.3
  96.7 1.7 %shard_map.86 = f32[2,8,32,512]{3,2,1,0:T(8,128)} custom-call(f32[2048,128]{1,0:T(8,128)S(1)} %bitcast.8, f32[8,32,512]{2,1,0:T(8,128)S(1)} %copy-done.3, bf16[512,256]{1,0:T(8,128)(2,1)S(1)} %copy-done.1, f32[8,128]{1,0:T(8,128)S(1)} %copy-done.2), custom_call_target="tpu_custom_call" | custom-call | flops 805306368 | bytes 4194304 | tf_op jit(solution)/shard_map/pallas_call | solution.py:359
  (1 shorter events, 0.0 us)
Async XLA Ops:
  0.0 50.6 %copy-start.2 = (f32[8,128]{1,0:T(8,128)S(1)}, f32[8,128]{1,0:T(8,128)}, u32[]{:S(2)}) copy-start(f32[8,128]{1,0:T(8,128)} %constant.18.clone.tw_hbm.tw_ref) | copy-start | bytes 12292
  3.3 47.3 %all-to-all-start = ((f32[256,8,128]{2,1,0:T(8,128)}), f32[256,8,128]{2,1,0:T(8,128)S(1)}, u32[]{:S(2)}, u32[]{:S(2)}) async-start(f32[256,8,128]{2,1,0:T(8,128)} %bitcast), calls=%async_computation | async-start | bytes 2097152 | tf_op jit(solution)/shard_map/all_to_all | solution.py:421
  25.8 24.8 %copy-start = (bf16[4352,256]{1,0:T(8,128)(2,1)S(1)}, bf16[4352,256]{1,0:T(8,128)(2,1)}, u32[]{:S(2)}) copy-start(bf16[4352,256]{1,0:T(8,128)(2,1)} %get-tuple-element.9.mix_ref) | copy-start | bytes 6684676
  25.8 0.8 copy-start.4
  32.5 64.2 %copy-start.1 = (bf16[512,256]{1,0:T(8,128)(2,1)S(1)}, bf16[512,256]{1,0:T(8,128)(2,1)}, u32[]{:S(2)}) copy-start(bf16[512,256]{1,0:T(8,128)(2,1)} %constant.17.clone.table_hbm.table_ref) | copy-start | bytes 786436
  50.6 46.1 %copy-start.3 = (f32[8,32,512]{2,1,0:T(8,128)S(1)}, f32[8,32,512]{2,1,0:T(8,128)}, u32[]{:S(2)}) copy-start(f32[8,32,512]{2,1,0:T(8,128)} %contrast_ref.1) | copy-start | bytes 1572868

commit v6 on v5

--- a/solution.py
+++ b/solution.py
@@ -274,7 +274,7 @@
         sums = sums[: 2 * PLANES] + sums[2 * PLANES :] + dot_nn(mix_ref[OWN_AT : OWN_AT + 2 * PLANES], x_lo)
         own[g, 0, :PLANES], own[g, 1, :PLANES] = sums[:PLANES], sums[PLANES:]
 
-    @pl.loop(0, 4)
+    @pl.loop(0, 4, unroll=2)
     def _(g):
         pltpu.make_async_copy(f_hbm.at[g], f_ref.at[g], sems.at[g]).wait()
 

time: 98.7 us -> 98.6 us (level)
  no operation moved by 1% of the time
where the time goes in v6:
time: 98.6 us; the launch traced here: 98.3 us
  blocking collectives  36.8 us (37%)
  Pallas kernels  24.5 us (25%)
  waiting for transfers between devices  18.1 us (18%)
  starting transfers between devices  15.7 us (16%)
  local copies, waits for them, and re-layouts  2.47 us (3%)
    all_to_all x1, blocking collectives, body(): lines = lax.all_to_all(lines.reshape(HALF, 8, 128), AXES, 0, 0, tiled=True)  36.8 us
    pallas_call x5, Pallas kernels, call(): pl.pallas_call(kernel, grid=grid, out_shape=out_shape, in_specs=in_specs,...  24.5 us
    all_to_all x1, waiting for transfers between devices, body(): lines = lax.all_to_all(sent.reshape(HALF, 8, 128), AXES, 0, 0, tiled=True)  18.1 us
    all_to_all x1, starting transfers between devices, body(): lines = lax.all_to_all(sent.reshape(HALF, 8, 128), AXES, 0, 0, tiled=True)  15.7 us
  transfers between devices with their start and end apart: 1, of which 1 were waited for; matrix products, arithmetic and copies ran while one was open for 2% of the time, Pallas kernels for 10%

profile of v6, /device:TPU:1, one launch (start us, length us, event | category | flops | bytes accessed | tf_op | source)
XLA Modules:
  0.0 98.3 jit_solution(2235505949042834848)
XLA Ops:
  0.0 0.0 copy-start.2
  0.0 3.2 %shard_map.82 = f32[2048,128]{1,0:T(8,128)} custom-call(f32[2,8,32,512]{3,2,1,0:T(8,128)} %w_hbm.1, bf16[512,256]{1,0:T(8,128)(2,1)} %constant.17.clone.table_hbm.table_ref, f32[8,128]{1,0:T(8,128)} %constant.18.clone.tw_hbm.tw_ref), custom_call_target="tpu_custom_call" | custom-call | flops 805306368 | bytes 4194304 | tf_op jit(solution)/shard_map/pallas_call | solution.py:359
  3.3 15.7 %all-to-all-start = ((f32[256,8,128]{2,1,0:T(8,128)}), f32[256,8,128]{2,1,0:T(8,128)S(1)}, u32[]{:S(2)}, u32[]{:S(2)}) async-start(f32[256,8,128]{2,1,0:T(8,128)} %bitcast), calls=%async_computation | async-start | bytes 2097152 | tf_op jit(solution)/shard_map/all_to_all | solution.py:421
  18.9 0.8 reverse
  19.8 0.1 slice
  19.9 0.7 pad.8.han_ref
  20.6 0.8 convert_reduce_fusion.start_ref
  21.4 4.5 %shard_map.83 = (bf16[4352,256]{1,0:T(8,128)(2,1)}, s32[8]{0:T(128)S(1)}) custom-call(s32[8]{0:T(128)S(1)} %convert_reduce_fusion.start_ref, f32[2,8,256]{2,1,0:T(8,128)S(1)} %pad.7.toe_ref, f32[2,8,256]{2,1,0:T(8,128)S(1)} %pad.8.han_ref), custom_call_target="tpu_custom_call" | custom-call | flops 1073741824 | bytes 4194304 | tf_op jit(solution)/shard_map/pallas_call | solution.py:359
  25.8 0.0 copy-start
  25.8 0.0 copy-start.4
  25.8 0.8 copy-done.4
  26.6 5.8 %shard_map.84 = (f32[4,3008,256]{2,1,0:T(8,128)}, f32[4,128,256]{2,1,0:T(8,128)}) custom-call(f32[8]{0:T(128)S(1)} %copy-done.4, s32[8]{0:T(128)S(1)} %get-tuple-element.10.start_ref, s32[1]{0:T(128)} %bitcast.2.ky_ref), custom_call_target="tpu_custom_call" | custom-call | flops 4294967296 | bytes 4194304 | tf_op jit(solution)/shard_map/pallas_call | solution.py:359
  32.5 0.0 copy-start.1
  32.5 18.1 %all-to-all-done = f32[256,8,128]{2,1,0:T(8,128)S(1)} async-done(((f32[256,8,128]{2,1,0:T(8,128)}), f32[256,8,128]{2,1,0:T(8,128)S(1)}, u32[]{:S(2)}, u32[]{:S(2)}) %all-to-all-start) | async-done | bytes 1048608 | tf_op jit(solution)/shard_map/all_to_all | solution.py:421
  50.6 0.0 copy-start.3
  50.6 0.0 copy-done.2
  50.6 0.0 copy-done
  50.6 9.2 %shard_map.85 = f32[16,16,8,128]{3,2,1,0:T(8,128)S(1)} custom-call(s32[8]{0:T(128)S(1)} %convert_reduce_fusion.start_ref, f32[16,16,8,128]{3,2,1,0:T(8,128)S(1)} %bitcast.6, bf16[512,256]{1,0:T(8,128)(2,1)} %constant.17.clone.table_hbm.table_ref, f32[8,128]{1,0:T(8,128)S(1)} %copy-done.2, bf16[4352,256]{1,0:T(8,128)(2,1)S(1)} %copy-done, ...), custom_call_target="tpu_custom_call" | custom-call | flops 4294967296 | bytes 4194304 | tf_op jit(solution)/shard_map/pallas_call | solution.py:359
  59.8 36.8 %all_to_all.10 = f32[256,8,128]{2,1,0:T(8,128)S(1)} all-to-all(f32[256,8,128]{2,1,0:T(8,128)S(1)} %bitcast.7), channel_id=1, replica_groups=mesh['lat'=16,'lay'=16] {'lay','lat'}, dimensions={0} | all-to-all | bytes 2097152 | tf_op jit(solution)/shard_map/all_to_all | solution.py:441
  96.6 0.0 copy-done.1
  96.6 0.0 copy-done.3
  96.6 1.7 %shard_map.86 = f32[2,8,32,512]{3,2,1,0:T(8,128)} custom-call(f32[2048,128]{1,0:T(8,128)S(1)} %bitcast.8, f32[8,32,512]{2,1,0:T(8,128)S(1)} %copy-done.3, bf16[512,256]{1,0:T(8,128)(2,1)S(1)} %copy-done.1, f32[8,128]{1,0:T(8,128)S(1)} %copy-done.2), custom_call_target="tpu_custom_call" | custom-call | flops 805306368 | bytes 4194304 | tf_op jit(solution)/shard_map/pallas_call | solution.py:359
  (1 shorter events, 0.0 us)
Async XLA Ops:
  0.0 50.6 %copy-start.2 = (f32[8,128]{1,0:T(8,128)S(1)}, f32[8,128]{1,0:T(8,128)}, u32[]{:S(2)}) copy-start(f32[8,128]{1,0:T(8,128)} %constant.18.clone.tw_hbm.tw_ref) | copy-start | bytes 12292
  3.3 47.3 %all-to-all-start = ((f32[256,8,128]{2,1,0:T(8,128)}), f32[256,8,128]{2,1,0:T(8,128)S(1)}, u32[]{:S(2)}, u32[]{:S(2)}) async-start(f32[256,8,128]{2,1,0:T(8,128)} %bitcast), calls=%async_computation | async-start | bytes 2097152 | tf_op jit(solution)/shard_map/all_to_all | solution.py:421
  25.8 24.8 %copy-start = (bf16[4352,256]{1,0:T(8,128)(2,1)S(1)}, bf16[4352,256]{1,0:T(8,128)(2,1)}, u32[]{:S(2)}) copy-start(bf16[4352,256]{1,0:T(8,128)(2,1)} %get-tuple-element.9.mix_ref) | copy-start | bytes 6684676
  25.8 0.8 copy-start.4
  32.5 64.1 %copy-start.1 = (bf16[512,256]{1,0:T(8,128)(2,1)S(1)}, bf16[512,256]{1,0:T(8,128)(2,1)}, u32[]{:S(2)}) copy-start(bf16[512,256]{1,0:T(8,128)(2,1)} %constant.17.clone.table_hbm.table_ref) | copy-start | bytes 786436
  50.6 46.0 %copy-start.3 = (f32[8,32,512]{2,1,0:T(8,128)S(1)}, f32[8,32,512]{2,1,0:T(8,128)}, u32[]{:S(2)}) copy-start(f32[8,32,512]{2,1,0:T(8,128)} %contrast_ref.1) | copy-start | bytes 1572868
